TPU v7x, 32 devices: a whole 2x2x4 slice. The times are simulated.
32 devices in a mesh: dp: 8 (over z, core), mp: 2 (over x), pre: 2 (over y).
Axes of the slice: x: 2, y: 2, z: 4, core: 2. Of those that a mesh axis runs over, the one named last changes fastest.
Arguments:
- activations: bfloat16 [12288, 1024], P('dp'), may hold values from -6 to 6
- grad_output: bfloat16 [12288, 4096], P('dp', ('mp', 'pre')), may hold values from -0.0546875 to 0.0546875
- left_old: float32 [1024, 1024], P(('mp', 'pre'), 'dp'), may hold values from -1 to 9, as said below
- right_old: float32 [4096, 4096], P(('mp', 'pre'), 'dp'), may hold values from -1 to 9, as said below
- probe_left: float32 [1024], replicated, may hold values from -6 to 6
- probe_right: float32 [4096], replicated, may hold values from -6 to 6
Outputs:
- left_new: float32 [1024, 1024], P(('mp', 'pre'), 'dp')
- right_new: float32 [4096, 4096], P(('mp', 'pre'), 'dp')
- update: float32 [1024, 4096], P('dp', ('mp', 'pre'))
Inputs may be any that keep to these rules, and one draw needn't show every extreme that they name: `left_old`: symmetric and positive definite. `right_old`: symmetric and positive definite.
All inputs are finite; a program needn't handle non-finite values.
Results may differ from a plain program's by a relative error of at most 0.0003.
Values sent between devices are 32-bit elements; how exact they have to be, the bound alone decides.
No kernel may reach another device: no remote copies, remote signals or barrier semaphores. Data moves between devices by JAX's collectives and lax.ppermute only.
A program may use at most 64 MiB of HBM per device.

v0:
```python
import jax
import jax.numpy as jnp
from jax import lax
from jax.experimental import pallas as pl
from jax.experimental.pallas import tpu as pltpu
from jax.sharding import Mesh, PartitionSpec as P

beta_decay = 0.9
norm_floor = 1e-06
count = 4

LINE, CORE, MP, PRE = "line", "core", "mp", "pre"
AXES = (LINE, CORE, MP, PRE)
f32, bf16 = jnp.float32, jnp.bfloat16


def halves(x):
    high = x.astype(bf16)
    return high, (x - high.astype(f32)).astype(bf16)


def whole_of(high, low):
    return high.astype(f32) + low.astype(f32)


def product(a, b, a_dim, b_dim):
    def one(x, y):
        return lax.dot_general(
            x, y, (((a_dim,), (b_dim,)), ((), ())), preferred_element_type=f32
        )

    return one(a[0], b[0]) + (one(a[0], b[1]) + one(a[1], b[0]))


def select_by(index, options):
    result = None
    for value, array in options.items():
        result = array if result is None else jnp.where(index == value, array, result)
    return result


def tie(values):
    return lax.optimization_barrier(tuple(values))


def call(body, outputs, numbers, arrays, space=pltpu.VMEM, scratch=(), mebibytes=24):
    inputs, results = len(arrays), len(outputs)

    def kernel(*refs):
        body(
            refs[0],
            refs[1 : 1 + inputs],
            refs[1 + inputs : 1 + inputs + results],
            *refs[1 + inputs + results :],
        )

    return pl.pallas_call(
        kernel,
        out_shape=[jax.ShapeDtypeStruct(shape, dtype) for shape, dtype in outputs],
        in_specs=[pl.BlockSpec(memory_space=pltpu.SMEM)]
        + [pl.BlockSpec(memory_space=space)] * inputs,
        out_specs=[pl.BlockSpec(memory_space=pltpu.VMEM)] * results,
        scratch_shapes=scratch,
        compiler_params=pltpu.CompilerParams(vmem_limit_bytes=mebibytes << 20),
        cost_estimate=pl.CostEstimate(flops=1, bytes_accessed=1, transcendentals=0),
    )(numbers, *arrays)


def added(numbers, arrays):
    def body(number, inputs, outputs):
        total = inputs[0][...]
        for array in inputs[1:]:
            total = total + array[...]
        outputs[0][...] = total

    return call(body, [(arrays[0].shape, f32)], numbers, arrays)[0]


def fetching(body, outputs, numbers, choices, shape, arrays=(), mebibytes=18):
    sources = []

    def place(array):
        for i, known in enumerate(sources):
            if known is array:
                return i
        sources.append(array)
        return len(sources) - 1

    shapes = [choice[2] if len(choice) > 2 else shape for choice in choices]
    choices = [
        (choice[0], {k: [(place(a), r) for a, r in terms] for k, terms in choice[1].items()})
        for choice in choices
    ]
    wholes = [place(array) for array in arrays]
    most = [max(1, *(len(t) for t in options.values())) for _, options in choices]
    many = len(choices)

    def inner(number, inputs, results, *scratch):
        held, kept = scratch[:many], scratch[many:-2]
        sems, kept_sems = scratch[-2:]

        def copies(o, terms):
            return [
                pltpu.make_async_copy(
                    inputs[a].at[pl.ds(r, shapes[o][0])], held[o].at[i], sems.at[o, i]
                )
                for i, (a, r) in enumerate(terms)
            ]

        loads = [
            pltpu.make_async_copy(inputs[a], kept[i], kept_sems.at[i])
            for i, a in enumerate(wholes)
        ]
        for o, (which, options) in enumerate(choices):
            for k, terms in options.items():

                @pl.when(number[which] == k)
                def _():
                    for copy in copies(o, terms):
                        copy.start()

        for copy in loads:
            copy.start()
        for o, (which, options) in enumerate(choices):
            for k, terms in options.items():

                @pl.when(number[which] == k)
                def _():
                    for copy in copies(o, terms):
                        copy.wait()
                    if not terms:
                        held[o][0] = jnp.zeros(shapes[o], f32)
                    if len(terms) > 1:
                        total = held[o][0]
                        for i in range(1, len(terms)):
                            total = total + held[o][i]
                        held[o][0] = total

        for copy in loads:
            copy.wait()
        body(number, [held[o].at[0] for o in range(many)], kept, results)

    return call(
        inner,
        outputs,
        numbers,
        sources,
        pl.ANY,
        [
            *[pltpu.VMEM((m,) + tuple(s), f32) for m, s in zip(most, shapes)],
            *[pltpu.VMEM(array.shape, array.dtype) for array in arrays],
            pltpu.SemaphoreType.DMA((max(many, 1), max(most + [1]))),
            pltpu.SemaphoreType.DMA((max(len(arrays), 1),)),
        ],
        mebibytes,
    )


def chosen_sums(numbers, choices, shape, more, tails):
    many = len(choices)
    sizes = [tail[2][0] for tail in tails] + [0] * (many - len(tails))
    arrays = []

    def place(array):
        for i, known in enumerate(arrays):
            if known is array:
                return i
        arrays.append(array)
        return len(arrays) - 1

    plans = [
        (choice[0], {k: [(place(a), r) for a, r in terms] for k, terms in choice[1].items()})
        for choice in choices + tails
    ]

    def body(number, inputs, outputs):
        def write(plan, result, at, rows):
            which, options = plan
            for k, terms in options.items():

                @pl.when(number[which] == k)
                def _():
                    total = jnp.zeros((rows,) + shape[1:], f32)
                    for i, (a, r) in enumerate(terms):
                        part = inputs[a][r : r + rows]
                        total = part if i == 0 else total + part
                    result[at : at + rows] = total

        for i, (result, rows, size) in enumerate(zip(outputs, more, sizes)):
            at = shape[0]
            write(plans[i], result, 0, at)
            if size:
                write(plans[many + i], result, at, size)
            if rows > size:
                result[at + size :] = jnp.zeros((rows - size,) + shape[1:], f32)

    out = [((shape[0] + rows,) + shape[1:], f32) for rows in more]
    return call(body, out, numbers, arrays, mebibytes=12)


class Windows:
    def __init__(self):
        self.now = 0
        self.processes = []

    def add(self, process):
        self.processes.append([process, None, None])

    def open(self):
        ended = []
        for entry in self.processes:
            process, due, values = entry
            if values and due >= self.now:
                continue
            try:
                windows, entry[2] = process.send(values)
                entry[1] = self.now + windows - 1
            except StopIteration:
                ended.append(entry)
        for entry in ended:
            self.processes.remove(entry)

    def close(self, *others):
        due = [entry for entry in self.processes if entry[1] == self.now and entry[2]]
        flat = list(others)
        for entry in due:
            flat.extend(entry[2])
        if flat:
            flat = list(tie(flat))
        at = len(others)
        for entry in due:
            size = len(entry[2])
            entry[2] = flat[at : at + size]
            at += size
        self.now += 1
        return flat[: len(others)]


def make_step(sizes):
    line, cores, mp, pre = (sizes[name] for name in AXES)
    models = mp * pre
    last = count - 1

    def swap(array, axis, bit):
        return lax.ppermute(array, axis, [(i, i ^ bit) for i in range(sizes[axis])])

    def bits(axis):
        return [1 << i for i in range(sizes[axis].bit_length() - 1)]

    def total(numbers, array, axes):
        for axis in axes:
            for bit in bits(axis):
                pair = yield 1, (array, swap(array, axis, bit))
                array = added(numbers, pair)
        return array

    def snake(array, outward):
        pairs = []
        for z in range(line):
            for c in range(cores):
                goal = z + (1 if (c == 0) == outward else -1)
                if 0 <= goal < line:
                    pairs.append((z * cores + c, goal * cores + c))
                else:
                    pairs.append((z * cores + c, z * cores + 1 - c))
        return lax.ppermute(array, (LINE, CORE), pairs)

    def shards(activations, grad_output, left_old, right_old, probe_left, probe_right):
        z, core = lax.axis_index(LINE), lax.axis_index(CORE)
        x, y = lax.axis_index(MP), lax.axis_index(PRE)
        model = x * pre + y
        width = activations.shape[1]
        block = grad_output.shape[1]
        hidden = block * models
        panel = block // cores
        own_rows = width // (line * cores)
        model_rows = width // models
        piece = width // count
        owner_x, owner_y = z // pre, z % pre
        there = jnp.where(core == 0, z, line - 1 - z)
        numbers = jnp.stack(
            [z, core, there, line - 1 - there, x == owner_x, y == owner_y, model]
        ).astype(jnp.int32)
        Z, C, THERE, BACK, IN_X, IN_Y, MODEL = range(7)
        shape = (piece, panel)
        windows = Windows()
        state = {}

        def to_partner(array):
            return swap(array, CORE, 1)

        def device(number):
            return number[Z] * cores + number[C]

        def local(first, end, mebibytes):
            rows = (end - first) * piece
            tokens = activations.shape[0]
            parts, slices = 4, 3
            span = tokens // parts
            thin = span // slices

            def body(number, inputs, outputs, left, right, sems):
                copies = []
                for i in range(parts):
                    for k in range(slices):
                        at = pl.ds(i * span + k * thin, thin)
                        copies.append(
                            pltpu.make_async_copy(
                                inputs[0].at[at, pl.ds(first * piece, rows)],
                                left.at[at],
                                sems.at[0, i, k],
                            )
                        )
                        copies.append(
                            pltpu.make_async_copy(
                                inputs[1].at[at], right.at[at], sems.at[1, i, k]
                            )
                        )
                for copy in copies:
                    copy.start()
                sums = [None] * (end - first)
                for i in range(parts):
                    for copy in copies[2 * slices * i : 2 * slices * (i + 1)]:
                        copy.wait()
                    at = slice(i * span, (i + 1) * span)
                    for j in range(end - first):
                        term = lax.dot_general(
                            left[at, j * piece : (j + 1) * piece],
                            right[at],
                            (((0,), (0,)), ((), ())),
                            preferred_element_type=f32,
                        )
                        sums[j] = term if i == 0 else sums[j] + term
                zeroth = jnp.full(shape, number[C], jnp.int32) == 0
                for j, both in enumerate(sums):
                    low, high = both[:, :panel], both[:, panel:]
                    outputs[0][j * piece : (j + 1) * piece] = jnp.where(zeroth, low, high)
                    outputs[1 + j][...] = jnp.where(zeroth, high, low)

            return call(
                body,
                [((rows, panel), f32)] + [(shape, f32)] * (end - first),
                numbers,
                [activations, grad_output],
                pl.ANY,
                [
                    pltpu.VMEM((tokens, rows), bf16),
                    pltpu.VMEM(grad_output.shape, bf16),
                    pltpu.SemaphoreType.DMA((2, parts, slices)),
                ],
                mebibytes,
            )

        kept_first, away = local(0, 1, 60)
        arrived = [to_partner(away)]

        class Chain:
            def __init__(self, terms):
                self.terms = terms
                self.sent, self.out, self.home, self.options = [], [], [], []

            def next_sums(self, t):
                choices = []
                for which, got in ((THERE, self.out), (BACK, self.home)):
                    options = {}
                    for k in range(line):
                        options[k] = []
                        if 0 <= t - k < count:
                            options[k] = self.terms(t - k)
                            if k:
                                options[k] = options[k] + [(got[t - 1], 0)]
                    choices.append((which, options))
                return choices

            def next_tails(self, t, piece_number, array):
                choices = []
                if not 0 <= t - piece_number < line:
                    return choices
                for which, got in ((THERE, self.out), (BACK, self.home)):
                    options = {k: [] for k in range(line)}
                    k = t - piece_number
                    options[k] = [(array, 0)] + ([(got[t - 1], piece)] if k else [])
                    choices.append((which, options, array.shape))
                return choices

            def finished_tail(self, piece_number, array):
                j = piece_number
                options = {
                    k: [(self.sent[j + k], piece), (self.home[j + line - 2 - k], piece)]
                    for k in range(line - 1)
                }
                options[line - 1] = [(array, 0), (self.out[j + line - 2], piece)]
                return THERE, options, array.shape

            def send(self, going_out, going_home):
                self.sent.append(going_out)
                self.out.append(snake(going_out, True))
                self.home.append(snake(going_home, False))

            def finished(self, t):
                j = t - (line - 1)
                if not 0 <= j < count:
                    return []
                options = {
                    k: [(self.sent[j + k], 0), (self.home[j + line - 2 - k], 0)]
                    for k in range(line - 1)
                }
                options[line - 1] = self.terms(j) + [(self.out[j + line - 2], 0)]
                self.options.append((THERE, options))
                return self.options[-1:]

        gradient = Chain(
            lambda j: [
                (kept_rest[0], (j - 1) * piece) if j else (kept_first, 0),
                (arrived[j], 0),
            ]
        )
        mixed = Chain(lambda j: [(state["kept", j], 0), (state["swapped", j], 0)])
        own, wishes, kept_rest = [], [], []

        def row(array):
            return array.reshape(1, -1)

        def exchange(array, axis):
            return total(numbers, array, (axis,))

        def placed(number, column):
            wide = (own_rows, width)
            at = lax.broadcasted_iota(jnp.int32, wide, 0) + device(number) * own_rows
            here = lax.broadcasted_iota(jnp.int32, wide, 1) == at
            return jnp.sum(jnp.where(here, column, 0.0), axis=0, keepdims=True)

        def panel_of(which):
            return row(lax.dynamic_slice_in_dim(probe_right, which * panel, panel, 0))

        def beside(first, second):
            def body(number, inputs, outputs):
                size = inputs[0].shape[1]
                outputs[0][:, :size] = inputs[0][...]
                outputs[0][:, size:] = inputs[1][...]

            shape = first.shape[0], first.shape[1] + second.shape[1]
            return call(body, [(shape, f32)], numbers, [first, second])[0]

        def left_turned():
            return (beta_decay * left_old).T

        block_rows, image_rows = block // panel, width // panel
        tail_rows = -(-(block_rows + image_rows) // 8) * 8
        tail_piece = 2

        def old_factors():
            while windows.now < 1:
                yield 1, ()

            def body(number, inputs, outputs):
                old = beta_decay * inputs[0][...]
                outputs[0][...], outputs[1][...] = halves(old)
                image = jnp.sum(old * inputs[1][...], axis=1, keepdims=True).T
                outputs[2][...] = jnp.zeros((tail_rows, panel), f32)
                for r in range(block_rows):
                    outputs[2][r : r + 1] = image[:, r * panel : (r + 1) * panel]
                image = jnp.sum(inputs[2][...] * inputs[3][...], axis=1, keepdims=True)
                image = placed(number, image)
                for r in range(image_rows):
                    at = block_rows + r
                    outputs[2][at : at + 1] = image[:, r * panel : (r + 1) * panel]

            own_probe = lax.dynamic_slice_in_dim(probe_left, model * model_rows, model_rows, 0)
            high, low, images = call(
                body,
                [((block, panel), bf16), ((block, panel), bf16), ((tail_rows, panel), f32)],
                numbers,
                [right_old, panel_of(z * cores + core), left_turned(), row(own_probe)],
            )
            *state["old"], state["tail"] = yield 1, (high, low, images)

        def old_left():
            while windows.now < 1:
                yield 1, ()
            rows = left_turned()
            for axis in (PRE, MP):
                for bit in bits(axis):
                    rows, got = yield 1, (rows, swap(rows, axis, bit))
                    rows = beside(rows, got)
            state["old_left"] = rows

        def spread(array, axis, place, owner):
            result = None
            size = sizes[axis]
            for s in range(1, size):
                got = lax.ppermute(array, axis, [(i, (i + s) % size) for i in range(size)])
                if result is None:
                    result = got
                else:
                    result = jnp.where((place - s) % size == owner, got, result)
            return result

        def panel_piece(j):
            while len(own) <= j:
                yield 1, ()
            if j < depth:
                other, got = yield 1, (to_partner(own[j]), spread(own[j], PRE, y, owner_y))
                state["other", j] = other, 0
            else:
                (got,) = yield 1, (spread(own[j], PRE, y, owner_y),)
            wishes.append((("held", j), (IN_Y, {1: [(own[j], 0)], 0: [(got, 0)]})))
            while ("held", j) not in state:
                yield 1, ()
            held = state["held", j]
            held, got = yield 1, (held, spread(held, MP, x, owner_x))
            riders = []
            if j + depth == last:
                while len(own) < count:
                    yield 1, ()
                riders = [*own[depth:], first_images()]

            def body(number, inputs, outputs):
                here = jnp.full(shape, number[IN_X], jnp.int32) == 1
                pair = halves(jnp.where(here, inputs[0][:piece], inputs[1][:piece]))
                outputs[0][...], outputs[1][...] = pair
                both = product(pair, (inputs[2][...], inputs[3][...]), 1, 1)
                low, high = both[:, :panel], both[:, panel:]
                zeroth = jnp.full(shape, number[C], jnp.int32) == 0
                outputs[2][...] = jnp.where(zeroth, low, high)
                outputs[3][:piece] = jnp.where(zeroth, high, low)
                at = piece
                for rider in inputs[4:]:
                    size = min(rider.shape[0], piece)
                    outputs[3][at : at + size] = rider[:size]
                    at += size

            away_rows = piece + sum(min(rider.shape[0], piece) for rider in riders)
            high, low, state["kept", j], away = call(
                body,
                [(shape, bf16), (shape, bf16), (shape, f32), ((away_rows, panel), f32)],
                numbers,
                [held, got, *state["old"], *riders],
            )
            state["panel", j] = high, low
            _, _, got = yield 1, (high, low, to_partner(away))
            state["swapped", j] = got
            if riders:
                for i in range(depth, count):
                    state["other", i] = got, (i - depth + 1) * piece
                state["images"] = riders[-1], got, (count - depth + 1) * piece

        depth = 2
        rider_rows = -(-(2 * image_rows + block_rows) // 8) * 8

        def first_images():
            def body(number, inputs, outputs):
                right, left = inputs[count][...], inputs[count + 1][...].T
                across = jnp.zeros((1, panel), f32)
                for j in range(count):
                    rows = slice(j * piece, (j + 1) * piece)
                    across += jnp.sum(inputs[j][:piece] * left[rows], axis=0, keepdims=True)
                old = inputs[count + 2][...]
                outputs[0][...] = jnp.zeros((rider_rows, panel), f32)
                outputs[0][2 * image_rows : 2 * image_rows + block_rows] = old[:block_rows]
                for i, vector in enumerate((right, across)):
                    image = jnp.concatenate(
                        [
                            jnp.sum(inputs[j][:piece] * vector, axis=1, keepdims=True).T
                            for j in range(count)
                        ],
                        axis=1,
                    )
                    for r in range(image_rows):
                        at = i * image_rows + r
                        part = image[:, r * panel : (r + 1) * panel]
                        if i:
                            part = part + hidden * old[block_rows + r : block_rows + r + 1]
                        outputs[0][at : at + 1] = part

            return call(
                body,
                [((rider_rows, panel), f32)],
                numbers,
                [
                    *own,
                    panel_of(model * cores + core),
                    row(probe_left),
                    state["old_images"],
                ],
            )[0]

        def over_models(array):
            steps = [(axis, bit) for axis in (PRE, MP) for bit in bits(axis)]
            for i, (axis, bit) in enumerate(steps):
                terms = yield 1, (array, swap(array, axis, bit))
                if i < len(steps) - 1:
                    array = added(numbers, terms)
            return terms

        def first_part(crossed):
            (crossed,) = yield 1, (crossed,)
            crossed = yield from over_models(crossed)
            while "squares" not in state:
                yield 1, ()

            def body(number, sums, inputs, outputs):
                top_left, top_right, scale = scales(inputs[6][...] + inputs[7][...])
                grad = inputs[4][...], inputs[5][...]
                rows = pl.ds(pl.multiple_of(device(number) * own_rows, own_rows), own_rows)
                own = whole_of(inputs[4][rows, :], inputs[5][rows, :])
                crossed = product(halves(inputs[0][...] + inputs[1][...]), grad, 1, 0)
                outputs[0][...] = scale * (
                    25.0 * own
                    - inputs[2][...] * (5.0 / top_left)
                    - (5.0 * inputs[3][...] - crossed / top_left) / top_right
                )

            (state["first_part"],) = fetching(
                body,
                [((own_rows, block), f32)],
                numbers,
                [],
                shape,
                [*crossed, *state["left_parts"], *state["block"], *state["squares"]],
            )

        def hold_block():
            state["block"] = yield 1, state["block"]

        def left_side():
            while ("other", last) not in state or "images" not in state:
                yield 1, ()
            other = [state["other", j] for j in range(count)]
            images, got, start = state["images"]

            def split_block(number, inputs, high, low):
                zeroth = jnp.full(shape, number[C], jnp.int32) == 0
                for j in range(count):
                    at = other[j][1]
                    mine, theirs = inputs[j][:piece], inputs[count + j][at : at + piece]
                    rows = pl.ds(j * piece, piece)
                    for i, part in enumerate(
                        (jnp.where(zeroth, mine, theirs), jnp.where(zeroth, theirs, mine))
                    ):
                        columns = pl.ds(i * panel, panel)
                        high[rows, columns], low[rows, columns] = halves(part)

            def body(number, inputs, outputs, high, low):
                split_block(number, inputs, high, low)
                rows = pl.ds(pl.multiple_of(device(number) * own_rows, own_rows), own_rows)
                gram = product((high[...], low[...]), (high[rows, :], low[rows, :]), 1, 1)
                outputs[0][:own_rows] = gram.T / hidden
                outputs[0][own_rows:] = jnp.zeros((8, width), f32)
                images = inputs[2 * count][...] + inputs[2 * count + 1][start:]
                for i in range(2):
                    for r in range(image_rows):
                        at = i * image_rows + r
                        outputs[0][own_rows + i : own_rows + i + 1, pl.ds(r * panel, panel)] = (
                            images[at : at + 1]
                        )
                for r in range(block_rows):
                    at = 2 * image_rows + r
                    outputs[1][:, pl.ds(r * panel, panel)] = images[at : at + 1]

            rows = (own_rows, width)
            sources = [*own, *(array for array, _ in other)]
            gram, state["old_image"] = call(
                body,
                [((own_rows + 8, width), f32), ((1, block), f32)],
                numbers,
                [*sources, images, got],
                scratch=[pltpu.VMEM((width, block), bf16)] * 2,
            )

            def body(number, inputs, outputs):
                split_block(number, inputs, *outputs)

            high, low = call(body, [((width, block), bf16)] * 2, numbers, sources)
            state["block"] = high, low
            windows.add(hold_block())
            gram = yield from over_models(gram)
            state["left_terms"] = gram

            def body(number, sums, inputs, outputs):
                gram = inputs[0][:own_rows] + inputs[1][:own_rows]
                old = []
                for m in range(models):
                    part = jnp.zeros((own_rows, model_rows), f32)
                    for k in range(models):
                        at = jnp.full(part.shape, number[MODEL], jnp.int32)
                        block_k = inputs[2][:, k * model_rows : (k + 1) * model_rows]
                        part = jnp.where(at == m ^ k, block_k, part)
                    old.append(part)
                left = jnp.concatenate(old, axis=1) + gram
                outputs[0][...] = left
                new = left[:, :model_rows]
                for m in range(1, models):
                    at = jnp.full(new.shape, number[MODEL], jnp.int32)
                    new = jnp.where(at == m, left[:, m * model_rows : (m + 1) * model_rows], new)
                outputs[4][...] = new.T
                grad = inputs[3][...], inputs[4][...]
                left_grad = product(halves(left), grad, 1, 0)
                outputs[1][...] = left_grad
                outputs[2][...] = gram
                outputs[3][...] = product(grad, halves(left_grad), 1, 1).T / width

            left, left_grad, gram, crossed, new = fetching(
                body,
                [(rows, f32), ((own_rows, block), f32), (rows, f32), (rows, f32)]
                + [((model_rows, own_rows), f32)],
                numbers,
                [],
                shape,
                [*gram, state["old_left"], *state["block"]],
            )
            state["left"] = left
            windows.add(first_part(crossed))
            left_grad, gram, left = yield 1, (left_grad, gram, left)
            partner_left = to_partner(left)

            def body(number, inputs, outputs):
                grad = inputs[1][...], inputs[2][...]
                outputs[0][...] = product(halves(inputs[0][...]), grad, 1, 0) * (hidden / width)

            (gram_grad,) = call(
                body, [((own_rows, block), f32)], numbers, [gram, *state["block"]]
            )
            state["partner_left"], *state["left_parts"] = yield 1, (
                partner_left,
                left_grad,
                gram_grad,
            )
            state["left_new"] = new

        def powers():
            while "left_terms" not in state:
                yield 1, ()

            def body(number, inputs, outputs):
                images = inputs[5][own_rows:] + inputs[6][own_rows:]
                outputs[1][...] = images[1:2] / hidden
                grad = whole_of(inputs[1][...], inputs[2][...])
                first = inputs[0][...] + (
                    jnp.sum(grad * images[0:1].T, axis=0, keepdims=True) / width
                )
                outputs[0][:, :width] = jnp.sum(grad * first, axis=1, keepdims=True).T
                old = whole_of(inputs[3][...], inputs[4][...])
                outputs[0][:, width : width + panel] = jnp.sum(
                    old * first.T, axis=0, keepdims=True
                )
                square = jnp.sum(first * first, axis=1, keepdims=True)
                outputs[0][:, width + panel :] = jnp.broadcast_to(square, (1, 128))

            joined, first = call(
                body,
                [((1, width + panel + 128), f32), ((1, width), f32)],
                numbers,
                [
                    state["old_image"],
                    *state["block"],
                    *state["old"],
                    *state["left_terms"],
                ],
            )
            for axis in (PRE, MP):
                for bit in bits(axis):
                    joined = added(numbers, [joined, swap(joined, axis, bit)])
            first, joined = yield 1, (first, joined)
            while "left" not in state or ("panel", last) not in state:
                yield 1, ()

            def body(number, inputs, outputs):
                joined = inputs[2 + 2 * count][...]
                for array in inputs[3 + 2 * count :]:
                    joined = joined + array[...]
                vector = joined[:, :width].T
                second = joined[:, width : width + panel]
                for j in range(count):
                    part = whole_of(inputs[2 + 2 * j][...], inputs[3 + 2 * j][...])
                    rows = vector[j * piece : (j + 1) * piece]
                    second = second + jnp.sum(part * rows, axis=0, keepdims=True) / width
                square = joined[:, width + panel : width + panel + 1]
                second = second / jnp.sqrt(square + norm_floor)
                right = jnp.sum(second * second, axis=1, keepdims=True)
                first = inputs[0][...]
                unit = first / jnp.sqrt(
                    jnp.sum(first * first, axis=1, keepdims=True) + norm_floor
                )
                second = jnp.sum(inputs[1][...] * unit, axis=1, keepdims=True)
                left = jnp.sum(second * second, axis=0, keepdims=True)
                spot = lax.broadcasted_iota(jnp.int32, (1, 128), 1)
                outputs[0][...] = jnp.where(spot == 0, left, right)

            panels = [half for j in range(count) for half in state["panel", j]]
            (squares,) = call(
                body,
                [((1, 128), f32)],
                numbers,
                [first, state["left"], *panels, joined],
            )
            squares = added(numbers, [squares, to_partner(squares)])
            for bit in bits(LINE)[:-2]:
                squares = added(numbers, [squares, swap(squares, LINE, bit)])
            squares = added(numbers, (yield 1, (squares, swap(squares, LINE, bits(LINE)[-2]))))
            state["squares"] = yield 1, (squares, swap(squares, LINE, bits(LINE)[-1]))

        def scales(squares):
            top = jnp.sqrt(squares + norm_floor)
            top_left, top_right = top[:, 0:1], top[:, 1:2]
            return top_left, top_right, 1.0 / (16.0 * jnp.sqrt(jnp.sqrt(top_left * top_right)))

        def right_factor():
            while ("panel", last) not in state or "block" not in state or windows.now < steps + 2:
                yield 1, ()

            def body(number, sums, inputs, outputs):
                pair = [
                    jnp.concatenate([inputs[3 + 2 * j + i][...] for j in range(count)], axis=0)
                    for i in range(2)
                ]
                gram = product((inputs[1][...], inputs[2][...]), pair, 0, 0)
                outputs[0][...] = beta_decay * inputs[0][...] + gram / width

            panels = [half for j in range(count) for half in state["panel", j]]
            (state["right_new"],) = yield 1, fetching(
                body,
                [((block, panel), f32)],
                numbers,
                [],
                shape,
                [right_old, *state["block"], *panels],
                32,
            )

        for j in range(count):
            windows.add(panel_piece(j))
        steps = count + line - 2
        def rows_here(number, i, rows, pieces):
            other = number[C] if i == 0 else 1 - number[C]
            at = jnp.full(rows.shape, number[Z] * cores + other, jnp.int32)
            for k in range(line * cores):
                j, start = divmod(k * own_rows, piece)
                for number_j, array in pieces:
                    if number_j == j:
                        rows = jnp.where(at == k, array[start : start + own_rows], rows)
            return rows

        def early_products():
            while len(mixed_wholes) < last or "partner_left" not in state:
                yield 1, ()

            def body(number, sums, inputs, outputs):
                pieces = [(j, inputs[2 + j]) for j in range(last)]
                pair = halves(jnp.concatenate([array[:piece] for _, array in pieces], axis=0))
                for i in range(2):
                    left = halves(inputs[i][:, : last * piece])
                    outputs[i][...] = product(left, pair, 1, 0)
                    outputs[2 + i][...] = rows_here(
                        number, i, jnp.zeros((own_rows, panel), f32), pieces
                    )

            state["early"] = yield 1, fetching(
                body,
                [((own_rows, panel), f32)] * 4,
                numbers,
                [],
                shape,
                [state["left"], state["partner_left"], *mixed_wholes],
            )

        mixed_wholes = []
        for process in (left_side, powers, right_factor, early_products):
            windows.add(process())

        for t in range(2 * steps):
            windows.open()
            current = gradient if t < steps else mixed
            choices = current.next_sums(t % steps) + gradient.finished(t)
            choices += mixed.finished(t - steps)
            names = [name for name, _ in wishes]
            choices += [choice for _, choice in wishes]
            wishes.clear()
            crowded = t == line + depth - 1
            longer = tail_rows + (16 if steps < t < steps + 3 else 8 if crowded else 0)
            extra = [longer] * 2 + [0] * (len(choices) - 2)
            for i, name in enumerate(names):
                extra[len(extra) - len(names) + i] = 8 if crowded else 0
            if crowded:
                extra[2] = 8
            if ("held", last) in names:
                extra[-1] = longer
            tails = []
            if t < steps and "tail" in state:
                tails = gradient.next_tails(t, tail_piece, state["tail"])
            results = list(chosen_sums(numbers, choices, shape, extra, tails))
            if t == 0:
                results[0], results[1], activations, grad_output, left_old, right_old = tie(
                    (*results, activations, grad_output, left_old, right_old)
                )
                windows.add(old_factors())
                windows.add(old_left())
                kept, *away = local(1, count, 40)
                kept_rest.append(kept)
                arrived += [to_partner(a) for a in away]
            current.send(*results[:2])
            for name in reversed(names):
                state[name] = results.pop()
            (own if len(own) < count else mixed_wholes).extend(results[2:])
            if t == tail_piece + line - 1:
                tail = gradient.finished_tail(tail_piece, state["tail"])

                def copy_body(number, sums, inputs, outputs):
                    outputs[0][...] = sums[0][...]

                (state["old_images"],) = fetching(
                    copy_body, [(tail[2], f32)], numbers, [tail], shape
                )
            windows.open()
            current.out[-1], current.home[-1] = windows.close(current.out[-1], current.home[-1])
        while windows.processes:
            windows.open()
            if windows.processes:
                windows.close()

        def body(number, sums, inputs, outputs):
            top_left, top_right, scale = scales(inputs[0][...] + inputs[1][...])
            pair = halves(sums[0][...])
            for i in range(2):
                rows = rows_here(number, i, inputs[6 + i][...], [(last, sums[0])])
                left = halves(inputs[2 + i][:, last * piece :])
                left = inputs[4 + i][...] + product(left, pair, 1, 0)
                outputs[i][...] = (left / top_left - 5.0 * rows) * (scale / top_right)

        mine, theirs = fetching(
            body,
            [((own_rows, panel), f32)] * 2,
            numbers,
            mixed.finished(steps),
            shape,
            [*state["squares"], state["left"], state["partner_left"], *state["early"]],
        )
        theirs = to_partner(theirs)

        def body(number, inputs, outputs):
            zeroth = jnp.full((own_rows, panel), number[C], jnp.int32) == 0
            mine, theirs = inputs[1][...], inputs[2][...]
            parts = jnp.where(zeroth, mine, theirs), jnp.where(zeroth, theirs, mine)
            for i, part in enumerate(parts):
                span = pl.ds(i * panel, panel)
                outputs[0][:, span] = inputs[0][:, span] + part

        (update,) = call(
            body, [((own_rows, block), f32)], numbers, [state["first_part"], mine, theirs]
        )
        return state["left_new"], state["right_new"], update

    return shards


def solution(mesh):
    dp, mp, pre = (mesh.shape[name] for name in ("dp", "mp", "pre"))
    cores = dp // (mp * pre)
    assert cores == 2
    split = Mesh(mesh.devices.reshape(dp // cores, cores, mp, pre), AXES)
    factor = P((MP, PRE), (LINE, CORE))
    in_specs = (
        P((LINE, CORE), None),
        P((LINE, CORE), (MP, PRE)),
        factor,
        factor,
        P(),
        P(),
    )
    out_specs = (factor, factor, P((LINE, CORE), (MP, PRE)))
    return jax.shard_map(
        make_step(dict(split.shape)),
        mesh=split,
        in_specs=in_specs,
        out_specs=out_specs,
        check_vma=False,
    )
```

profile of v0, /device:TPU:1, one launch (start us, length us, event | category | flops | bytes accessed | tf_op | source)
XLA Modules:
  0.0 221.5 jit_solution(6521119382611522252)
XLA Ops:
  1.3 4.9 %shard_map.85 = (f32[256,512]{1,0:T(8,128)}, f32[256,512]{1,0:T(8,128)}) custom-call(s32[7]{0:T(128)} %stack.39.refs_0_, bf16[1536,1024]{1,0:T(8,128)(2,1)} %refs_1_.2, bf16[1536,1024]{1,0:T(8,128)(2,1)} %refs_2_.2), custom_call_target="tpu_custom_call" | custom-call | flops 1 | bytes 1 | tf_op jit(solution)/shard_map/pallas_call | solution.py:57
  6.4 2.1 collective-permute-done.refs_2_.refs_4_.refs_6_.refs_7_
  10.4 2.4 %collective-permute-start.5 = (f32[264,512]{1,0:T(8,128)S(1)}, f32[264,512]{1,0:T(8,128)S(1)}, u32[]{:S(2)}, u32[]{:S(2)}) collective-permute-start(f32[264,512]{1,0:T(8,128)S(1)} %get-tuple-element.174), channel_id=1, source_target_pairs={{0,4},{4,12},{8,0},{12,20},{16,8},{20,28},{24,16},{28,24},{1,5},{5... | collective-permute-start | bytes 1622024 | tf_op jit(solution)/shard_map/ppermute | solution.py:266
  16.6 5.7 %shard_map.87 = (f32[768,512]{1,0:T(8,128)S(1)}, f32[256,512]{1,0:T(8,128)S(1)}, f32[256,512]{1,0:T(8,128)}, f32[256,512]{1,0:T(8,128)S(1)}) custom-call(s32[7]{0:T(128)S(1)} %copy-done.10, bf16[1536,1024]{1,0:T(8,128)(2,1)S(1)} %copy-done, bf16[1536,1024]{1,0:T(8,128)(2,1)S(1)} %copy-done.1), custom_call_target="tpu_custom_call" | custom-call | flops 1 | bytes 1 | tf_op jit(solution)/shard_map/pallas_call | solution.py:57
  35.8 5.1 %collective-permute-done.7.refs_7_.refs_11_ = f32[264,512]{1,0:T(8,128)} collective-permute-done((f32[264,512]{1,0:T(8,128)}, f32[264,512]{1,0:T(8,128)}, u32[]{:S(2)}, u32[]{:S(2)}) %collective-permute-start.7) | collective-permute-done | bytes 540704 | tf_op jit(solution)/shard_map/ppermute | solution.py:266
  49.0 6.5 %collective-permute-done.11.refs_2_ = f32[128,512]{1,0:T(8,128)S(1)} collective-permute-done((f32[128,512]{1,0:T(8,128)S(1)}, f32[128,512]{1,0:T(8,128)S(1)}, u32[]{:S(2)}, u32[]{:S(2)}) %collective-permute-start.11) | collective-permute-done | bytes 262176 | tf_op jit(solution)/shard_map/ppermute | solution.py:245
  55.5 2.0 collective-permute-done.10.refs_8_.refs_9_.refs_10_.refs_6_
  64.9 8.7 %collective-permute-done.15.refs_13_ = f32[256,512]{1,0:T(8,128)S(1)} collective-permute-done((f32[256,512]{1,0:T(8,128)S(1)}, f32[256,512]{1,0:T(8,128)S(1)}, u32[]{:S(2)}, u32[]{:S(2)}) %collective-permute-start.15) | collective-permute-done | bytes 524320 | tf_op jit(solution)/shard_map/ppermute | solution.py:492
  80.4 2.6 %collective-permute-start.19 = (f32[256,512]{1,0:T(8,128)S(1)}, f32[256,512]{1,0:T(8,128)S(1)}, u32[]{:S(2)}, u32[]{:S(2)}) collective-permute-start(f32[256,512]{1,0:T(8,128)S(1)} %get-tuple-element.202.refs_11_.refs_2_), channel_id=1, source_target_pairs={{0,4},{4,0},{1,5},{5,1},{2,6},{6,2},{3,7},{7,3},{8,12},{12,8},{9,1... | collective-permute-start | bytes 1572872 | tf_op jit(solution)/shard_map/ppermute | solution.py:245
  83.0 6.3 %collective-permute-done.18.refs_2_ = f32[256,512]{1,0:T(8,128)S(1)} collective-permute-done((f32[256,512]{1,0:T(8,128)S(1)}, f32[256,512]{1,0:T(8,128)S(1)}, u32[]{:S(2)}, u32[]{:S(2)}) %collective-permute-start.18) | collective-permute-done | bytes 524320 | tf_op jit(solution)/shard_map/ppermute | solution.py:492
  91.8 2.7 %collective-permute-start.21 = (f32[272,512]{1,0:T(8,128)S(1)}, f32[272,512]{1,0:T(8,128)S(1)}, u32[]{:S(2)}, u32[]{:S(2)}) collective-permute-start(f32[272,512]{1,0:T(8,128)S(1)} %get-tuple-element.211.refs_7_), channel_id=1, source_target_pairs={{0,8},{4,0},{8,16},{12,4},{16,24},{20,12},{24,28},{28,20},{1,9},{5... | collective-permute-start | bytes 1671176 | tf_op jit(solution)/shard_map/ppermute | solution.py:266
  97.6 2.6 %collective-permute-start.23 = (f32[256,512]{1,0:T(8,128)S(1)}, f32[256,512]{1,0:T(8,128)S(1)}, u32[]{:S(2)}, u32[]{:S(2)}) collective-permute-start(f32[256,512]{1,0:T(8,128)S(1)} %get-tuple-element.215), channel_id=1, source_target_pairs={{0,4},{4,0},{1,5},{5,1},{2,6},{6,2},{3,7},{7,3},{8,12},{12,8},{9,1... | collective-permute-start | bytes 1572872 | tf_op jit(solution)/shard_map/ppermute | solution.py:245
  101.7 4.6 %collective-permute-done.24.refs_2_ = f32[264,512]{1,0:T(8,128)S(1)} collective-permute-done((f32[264,512]{1,0:T(8,128)S(1)}, f32[264,512]{1,0:T(8,128)S(1)}, u32[]{:S(2)}, u32[]{:S(2)}) %collective-permute-start.24) | collective-permute-done | bytes 540704 | tf_op jit(solution)/shard_map/ppermute | solution.py:492
  110.6 3.0 %collective-permute-start.28 = (f32[776,512]{1,0:T(8,128)S(1)}, f32[776,512]{1,0:T(8,128)S(1)}, u32[]{:S(2)}, u32[]{:S(2)}) collective-permute-start(f32[776,512]{1,0:T(8,128)S(1)} %get-tuple-element.229), channel_id=1, source_target_pairs={{0,4},{4,0},{1,5},{5,1},{2,6},{6,2},{3,7},{7,3},{8,12},{12,8},{9,1... | collective-permute-start | bytes 4767752 | tf_op jit(solution)/shard_map/ppermute | solution.py:245
  116.7 9.2 %collective-permute-done.29.refs_2_ = f32[256,512]{1,0:T(8,128)S(1)} collective-permute-done((f32[256,512]{1,0:T(8,128)S(1)}, f32[256,512]{1,0:T(8,128)S(1)}, u32[]{:S(2)}, u32[]{:S(2)}) %collective-permute-start.29) | collective-permute-done | bytes 524320 | tf_op jit(solution)/shard_map/ppermute | solution.py:492
  128.2 1.9 collective-permute-start.32
  131.0 3.8 %shard_map.102 = (f32[136,1024]{1,0:T(8,128)S(1)}, f32[1,1024]{1,0:T(1,128)S(1)}) custom-call(s32[7]{0:T(128)S(1)} %copy-done.10, f32[256,512]{1,0:T(8,128)S(1)} %get-tuple-element.195.refs_12_.refs_1_, f32[256,512]{1,0:T(8,128)S(1)} %get-tuple-element.202.refs_11_.refs_2_, f32[264,512]{1,0:T(8,128)S(1)} %get-tuple-element.217.refs_12_.refs_3_.refs_5_, ...), custom_call_target="tpu_custom_call" | custom-call | flops 1 | bytes 1 | tf_op jit(solution)/shard_map/pallas_call | solution.py:57
  137.8 2.3 %collective-permute-start.33 = (f32[256,512]{1,0:T(8,128)S(1)}, f32[256,512]{1,0:T(8,128)S(1)}, u32[]{:S(2)}, u32[]{:S(2)}) collective-permute-start(f32[256,512]{1,0:T(8,128)S(1)} %get-tuple-element.243), channel_id=1, source_target_pairs={{0,4},{4,0},{1,5},{5,1},{2,6},{6,2},{3,7},{7,3},{8,12},{12,8},{9,1... | collective-permute-start | bytes 1572872 | tf_op jit(solution)/shard_map/ppermute | solution.py:245
  141.7 5.3 %collective-permute-done.35.refs_2_ = f32[136,1024]{1,0:T(8,128)S(1)} collective-permute-done((f32[136,1024]{1,0:T(8,128)S(1)}, f32[136,1024]{1,0:T(8,128)S(1)}, u32[]{:S(2)}, u32[]{:S(2)}) %collective-permute-start.35) | collective-permute-done | bytes 557088 | tf_op jit(solution)/shard_map/ppermute | solution.py:245
  148.7 2.0 collective-permute-start.36
  154.3 2.3 %collective-permute-start.38 = (f32[256,512]{1,0:T(8,128)S(1)}, f32[256,512]{1,0:T(8,128)S(1)}, u32[]{:S(2)}, u32[]{:S(2)}) collective-permute-start(f32[256,512]{1,0:T(8,128)S(1)} %get-tuple-element.259), channel_id=1, source_target_pairs={{0,4},{4,0},{1,5},{5,1},{2,6},{6,2},{3,7},{7,3},{8,12},{12,8},{9,1... | collective-permute-start | bytes 1572872 | tf_op jit(solution)/shard_map/ppermute | solution.py:245
  156.6 6.0 %shard_map.107 = f32[1024,512]{1,0:T(8,128)} custom-call(s32[7]{0:T(128)S(1)} %copy-done.10, f32[1024,512]{1,0:T(8,128)S(1)} %copy-done.7, bf16[1024,1024]{1,0:T(8,128)(2,1)S(1)} %get-tuple-element.266.refs_2_.refs_4_.refs_5_, bf16[1024,1024]{1,0:T(8,128)(2,1)S(1)} %get-tuple-element.267.refs_3_.refs_5_.refs_6_, ...), custom_call_target="tpu_custom_call" | custom-call | flops 1 | bytes 1 | tf_op jit(solution)/shard_map/pallas_call | solution.py:57
  164.9 2.6 %collective-permute-start.40 = (f32[264,512]{1,0:T(8,128)S(1)}, f32[264,512]{1,0:T(8,128)S(1)}, u32[]{:S(2)}, u32[]{:S(2)}) collective-permute-start(f32[264,512]{1,0:T(8,128)S(1)} %get-tuple-element.274.refs_12_.refs_8_.refs_1_), channel_id=1, source_target_pairs={{0,8},{4,0},{8,16},{12,4},{16,24},{20,12},{24,28},{28,20},{1,9},{5... | collective-permute-start | bytes 1622024 | tf_op jit(solution)/shard_map/ppermute | solution.py:266
  167.5 2.4 %shard_map.111 = (f32[1,1664]{1,0:T(1,128)S(1)}, f32[1,1024]{1,0:T(1,128)S(1)}) custom-call(s32[7]{0:T(128)S(1)} %copy-done.10, f32[1,1024]{1,0:T(1,128)S(1)} %get-tuple-element.279.refs_1_, bf16[1024,1024]{1,0:T(8,128)(2,1)S(1)} %get-tuple-element.266.refs_2_.refs_4_.refs_5_, bf16[1024,1024]{1,0:T(8,128)(2,1)S(1)} %get-tuple-element.267.refs_3_.refs_5_.refs_6_, ...), custom_call_target="tpu_custom_call" | custom-call | flops 1 | bytes 1 | tf_op jit(solution)/shard_map/pallas_call | solution.py:57
  175.3 4.4 %shard_map.109 = (f32[128,1024]{1,0:T(8,128)S(1)}, f32[128,1024]{1,0:T(8,128)S(1)}, f32[128,1024]{1,0:T(8,128)S(1)}, f32[128,1024]{1,0:T(8,128)S(1)}, f32[256,128]{1,0:T(8,128)}) custom-call(s32[7]{0:T(128)S(1)} %copy-done.10, f32[136,1024]{1,0:T(8,128)S(1)} %shard_map.106.refs_1_.refs_6_, f32[136,1024]{1,0:T(8,128)S(1)} %collective-permute-done.39.refs_2_.refs_7_, ...), custom_call_target="tpu_custom_call" | custom-call | flops 1 | bytes 1 | tf_op jit(solution)/shard_map/pallas_call | solution.py:57
  182.4 2.0 collective-permute-start.44
  184.3 2.0 collective-permute-start.46
  192.1 2.7 %collective-permute-done.48.refs_2_ = f32[1,128]{1,0:T(1,128)S(1)} collective-permute-done((f32[1,128]{1,0:T(1,128)S(1)}, f32[1,128]{1,0:T(1,128)S(1)}, u32[]{:S(2)}, u32[]{:S(2)}) %collective-permute-start.48) | collective-permute-done | bytes 544 | tf_op jit(solution)/shard_map/ppermute | solution.py:245
  194.8 5.1 %collective-permute-done.49.refs_2_ = f32[128,1024]{1,0:T(8,128)S(1)} collective-permute-done((f32[128,1024]{1,0:T(8,128)S(1)}, f32[128,1024]{1,0:T(8,128)S(1)}, u32[]{:S(2)}, u32[]{:S(2)}) %collective-permute-start.49) | collective-permute-done | bytes 524320 | tf_op jit(solution)/shard_map/ppermute | solution.py:245
  202.8 2.0 collective-permute-start.52
  206.6 8.8 %collective-permute-done.52.refs_8_.refs_11_ = f32[1,128]{1,0:T(1,128)S(1)} collective-permute-done((f32[1,128]{1,0:T(1,128)S(1)}, f32[1,128]{1,0:T(1,128)S(1)}, u32[]{:S(2)}, u32[]{:S(2)}) %collective-permute-start.52) | collective-permute-done | bytes 544 | tf_op jit(solution)/shard_map/ppermute | solution.py:245
  218.0 2.1 shard_map.122.refs_1_
  (157 shorter events, 94.3 us)
Async XLA Ops:
  10.4 13.7 %collective-permute-start.5 = (f32[264,512]{1,0:T(8,128)S(1)}, f32[264,512]{1,0:T(8,128)S(1)}, u32[]{:S(2)}, u32[]{:S(2)}) collective-permute-start(f32[264,512]{1,0:T(8,128)S(1)} %get-tuple-element.174), channel_id=1, source_target_pairs={{0,4},{4,12},{8,0},{12,20},{16,8},{20,28},{24,16},{28,24},{1,5},{5... | collective-permute-start | bytes 1622024 | tf_op jit(solution)/shard_map/ppermute | solution.py:266
  12.8 13.1 %collective-permute-start.4 = (f32[264,512]{1,0:T(8,128)S(1)}, f32[264,512]{1,0:T(8,128)S(1)}, u32[]{:S(2)}, u32[]{:S(2)}) collective-permute-start(f32[264,512]{1,0:T(8,128)S(1)} %get-tuple-element.173.refs_9_), channel_id=1, source_target_pairs={{0,8},{4,0},{8,16},{12,4},{16,24},{20,12},{24,28},{28,20},{1,9},{5... | collective-permute-start | bytes 1622024 | tf_op jit(solution)/shard_map/ppermute | solution.py:266
  27.6 13.4 %collective-permute-start.7 = (f32[264,512]{1,0:T(8,128)}, f32[264,512]{1,0:T(8,128)}, u32[]{:S(2)}, u32[]{:S(2)}) collective-permute-start(f32[264,512]{1,0:T(8,128)} %get-tuple-element.178), channel_id=1, source_target_pairs={{0,4},{4,12},{8,0},{12,20},{16,8},{20,28},{24,16},{28,24},{1,5},{5... | collective-permute-start | bytes 1622024 | tf_op jit(solution)/shard_map/ppermute | solution.py:266
  29.4 13.4 %collective-permute-start.6 = (f32[264,512]{1,0:T(8,128)}, f32[264,512]{1,0:T(8,128)}, u32[]{:S(2)}, u32[]{:S(2)}) collective-permute-start(f32[264,512]{1,0:T(8,128)} %get-tuple-element.177.refs_10_.refs_7_), channel_id=1, source_target_pairs={{0,8},{4,0},{8,16},{12,4},{16,24},{20,12},{24,28},{28,20},{1,9},{5... | collective-permute-start | bytes 1622024 | tf_op jit(solution)/shard_map/ppermute | solution.py:266
  29.4 13.4 %collective-permute-start.2 = (f32[256,512]{1,0:T(8,128)}, f32[256,512]{1,0:T(8,128)S(1)}, u32[]{:S(2)}, u32[]{:S(2)}) collective-permute-start(f32[256,512]{1,0:T(8,128)} %get-tuple-element.171), channel_id=1, source_target_pairs={{0,4},{4,0},{1,5},{5,1},{2,6},{6,2},{3,7},{7,3},{8,12},{12,8},{9,1... | collective-permute-start | bytes 1572872 | tf_op jit(solution)/shard_map/ppermute | solution.py:245
  44.3 13.2 %collective-permute-start.10 = (f32[264,512]{1,0:T(8,128)S(1)}, f32[264,512]{1,0:T(8,128)S(1)}, u32[]{:S(2)}, u32[]{:S(2)}) collective-permute-start(f32[264,512]{1,0:T(8,128)S(1)} %get-tuple-element.188), channel_id=1, source_target_pairs={{0,4},{4,12},{8,0},{12,20},{16,8},{20,28},{24,16},{28,24},{1,5},{5... | collective-permute-start | bytes 1622024 | tf_op jit(solution)/shard_map/ppermute | solution.py:266
  46.2 13.0 %collective-permute-start.9 = (f32[264,512]{1,0:T(8,128)S(1)}, f32[264,512]{1,0:T(8,128)S(1)}, u32[]{:S(2)}, u32[]{:S(2)}) collective-permute-start(f32[264,512]{1,0:T(8,128)S(1)} %get-tuple-element.187.refs_12_.refs_8_.refs_6_.refs_1_), channel_id=1, source_target_pairs={{0,8},{4,0},{8,16},{12,4},{16,24},{20,12},{24,28},{28,20},{1,9},{5... | collective-permute-start | bytes 1622024 | tf_op jit(solution)/shard_map/ppermute | solution.py:266
  46.2 13.0 %collective-permute-start.1 = (f32[256,512]{1,0:T(8,128)S(1)}, f32[256,512]{1,0:T(8,128)S(1)}, u32[]{:S(2)}, u32[]{:S(2)}) collective-permute-start(f32[256,512]{1,0:T(8,128)S(1)} %copy-done.15), channel_id=1, source_target_pairs={{0,4},{4,0},{1,5},{5,1},{2,6},{6,2},{3,7},{7,3},{8,12},{12,8},{9,1... | collective-permute-start | bytes 1572872 | tf_op jit(solution)/shard_map/ppermute | solution.py:245
  60.8 12.8 %collective-permute-start.13 = (f32[264,512]{1,0:T(8,128)S(1)}, f32[264,512]{1,0:T(8,128)S(1)}, u32[]{:S(2)}, u32[]{:S(2)}) collective-permute-start(f32[264,512]{1,0:T(8,128)S(1)} %get-tuple-element.194), channel_id=1, source_target_pairs={{0,4},{4,12},{8,0},{12,20},{16,8},{20,28},{24,16},{28,24},{1,5},{5... | collective-permute-start | bytes 1622024 | tf_op jit(solution)/shard_map/ppermute | solution.py:266
  61.6 13.9 %collective-permute-start.12 = (f32[264,512]{1,0:T(8,128)S(1)}, f32[264,512]{1,0:T(8,128)S(1)}, u32[]{:S(2)}, u32[]{:S(2)}) collective-permute-start(f32[264,512]{1,0:T(8,128)S(1)} %get-tuple-element.193.refs_10_.refs_7_.refs_3_), channel_id=1, source_target_pairs={{0,8},{4,0},{8,16},{12,4},{16,24},{20,12},{24,28},{28,20},{1,9},{5... | collective-permute-start | bytes 1622024 | tf_op jit(solution)/shard_map/ppermute | solution.py:266
  77.2 13.1 %collective-permute-start.17 = (f32[264,512]{1,0:T(8,128)S(1)}, f32[264,512]{1,0:T(8,128)S(1)}, u32[]{:S(2)}, u32[]{:S(2)}) collective-permute-start(f32[264,512]{1,0:T(8,128)S(1)} %get-tuple-element.200), channel_id=1, source_target_pairs={{0,4},{4,12},{8,0},{12,20},{16,8},{20,28},{24,16},{28,24},{1,5},{5... | collective-permute-start | bytes 1622024 | tf_op jit(solution)/shard_map/ppermute | solution.py:266
  77.2 13.5 %collective-permute-start.16 = (f32[264,512]{1,0:T(8,128)S(1)}, f32[264,512]{1,0:T(8,128)S(1)}, u32[]{:S(2)}, u32[]{:S(2)}) collective-permute-start(f32[264,512]{1,0:T(8,128)S(1)} %get-tuple-element.199.refs_9_.refs_5_), channel_id=1, source_target_pairs={{0,8},{4,0},{8,16},{12,4},{16,24},{20,12},{24,28},{28,20},{1,9},{5... | collective-permute-start | bytes 1622024 | tf_op jit(solution)/shard_map/ppermute | solution.py:266
  91.8 14.5 %collective-permute-start.22 = (f32[272,512]{1,0:T(8,128)S(1)}, f32[272,512]{1,0:T(8,128)S(1)}, u32[]{:S(2)}, u32[]{:S(2)}) collective-permute-start(f32[272,512]{1,0:T(8,128)S(1)} %get-tuple-element.212), channel_id=1, source_target_pairs={{0,4},{4,12},{8,0},{12,20},{16,8},{20,28},{24,16},{28,24},{1,5},{5... | collective-permute-start | bytes 1671176 | tf_op jit(solution)/shard_map/ppermute | solution.py:266
  91.8 14.5 %collective-permute-start.21 = (f32[272,512]{1,0:T(8,128)S(1)}, f32[272,512]{1,0:T(8,128)S(1)}, u32[]{:S(2)}, u32[]{:S(2)}) collective-permute-start(f32[272,512]{1,0:T(8,128)S(1)} %get-tuple-element.211.refs_7_), channel_id=1, source_target_pairs={{0,8},{4,0},{8,16},{12,4},{16,24},{20,12},{24,28},{28,20},{1,9},{5... | collective-permute-start | bytes 1671176 | tf_op jit(solution)/shard_map/ppermute | solution.py:266
  110.6 16.9 %collective-permute-start.28 = (f32[776,512]{1,0:T(8,128)S(1)}, f32[776,512]{1,0:T(8,128)S(1)}, u32[]{:S(2)}, u32[]{:S(2)}) collective-permute-start(f32[776,512]{1,0:T(8,128)S(1)} %get-tuple-element.229), channel_id=1, source_target_pairs={{0,4},{4,0},{1,5},{5,1},{2,6},{6,2},{3,7},{7,3},{8,12},{12,8},{9,1... | collective-permute-start | bytes 4767752 | tf_op jit(solution)/shard_map/ppermute | solution.py:245
  113.5 13.5 %collective-permute-start.27 = (f32[264,512]{1,0:T(8,128)S(1)}, f32[264,512]{1,0:T(8,128)S(1)}, u32[]{:S(2)}, u32[]{:S(2)}) collective-permute-start(f32[264,512]{1,0:T(8,128)S(1)} %get-tuple-element.223), channel_id=1, source_target_pairs={{0,4},{4,12},{8,0},{12,20},{16,8},{20,28},{24,16},{28,24},{1,5},{5... | collective-permute-start | bytes 1622024 | tf_op jit(solution)/shard_map/ppermute | solution.py:266
  113.5 13.9 %collective-permute-start.26 = (f32[264,512]{1,0:T(8,128)S(1)}, f32[264,512]{1,0:T(8,128)S(1)}, u32[]{:S(2)}, u32[]{:S(2)}) collective-permute-start(f32[264,512]{1,0:T(8,128)S(1)} %get-tuple-element.222.refs_11_), channel_id=1, source_target_pairs={{0,8},{4,0},{8,16},{12,4},{16,24},{20,12},{24,28},{28,20},{1,9},{5... | collective-permute-start | bytes 1622024 | tf_op jit(solution)/shard_map/ppermute | solution.py:266
  128.2 18.8 %collective-permute-start.32 = (f32[280,512]{1,0:T(8,128)S(1)}, f32[280,512]{1,0:T(8,128)S(1)}, u32[]{:S(2)}, u32[]{:S(2)}) collective-permute-start(f32[280,512]{1,0:T(8,128)S(1)} %get-tuple-element.240), channel_id=1, source_target_pairs={{0,4},{4,12},{8,0},{12,20},{16,8},{20,28},{24,16},{28,24},{1,5},{5... | collective-permute-start | bytes 1720328 | tf_op jit(solution)/shard_map/ppermute | solution.py:266
  130.1 16.9 %collective-permute-start.34 = (f32[280,512]{1,0:T(8,128)S(1)}, f32[280,512]{1,0:T(8,128)S(1)}, u32[]{:S(2)}, u32[]{:S(2)}) collective-permute-start(f32[280,512]{1,0:T(8,128)S(1)} %get-tuple-element.255.refs_1_), channel_id=1, source_target_pairs={{0,2},{2,0},{1,3},{3,1},{4,6},{6,4},{5,7},{7,5},{8,10},{10,8},{9,1... | collective-permute-start | bytes 1720328 | tf_op jit(solution)/shard_map/ppermute | solution.py:492
  130.4 16.6 %collective-permute-start.31 = (f32[280,512]{1,0:T(8,128)S(1)}, f32[280,512]{1,0:T(8,128)S(1)}, u32[]{:S(2)}, u32[]{:S(2)}) collective-permute-start(f32[280,512]{1,0:T(8,128)S(1)} %get-tuple-element.239.refs_12_.refs_9_), channel_id=1, source_target_pairs={{0,8},{4,0},{8,16},{12,4},{16,24},{20,12},{24,28},{28,20},{1,9},{5... | collective-permute-start | bytes 1720328 | tf_op jit(solution)/shard_map/ppermute | solution.py:266
  134.8 12.2 %collective-permute-start.35 = (f32[136,1024]{1,0:T(8,128)S(1)}, f32[136,1024]{1,0:T(8,128)S(1)}, u32[]{:S(2)}, u32[]{:S(2)}) collective-permute-start(f32[136,1024]{1,0:T(8,128)S(1)} %get-tuple-element.260.refs_1_), channel_id=1, source_target_pairs={{0,1},{1,0},{2,3},{3,2},{4,5},{5,4},{6,7},{7,6},{8,9},{9,8},{10,11... | collective-permute-start | bytes 1671176 | tf_op jit(solution)/shard_map/ppermute | solution.py:245
  147.7 15.7 %collective-permute-start.37 = (f32[280,512]{1,0:T(8,128)S(1)}, f32[280,512]{1,0:T(8,128)S(1)}, u32[]{:S(2)}, u32[]{:S(2)}) collective-permute-start(f32[280,512]{1,0:T(8,128)S(1)} %get-tuple-element.254), channel_id=1, source_target_pairs={{0,4},{4,12},{8,0},{12,20},{16,8},{20,28},{24,16},{28,24},{1,5},{5... | collective-permute-start | bytes 1720328 | tf_op jit(solution)/shard_map/ppermute | solution.py:266
  148.7 14.8 %collective-permute-start.36 = (f32[280,512]{1,0:T(8,128)S(1)}, f32[280,512]{1,0:T(8,128)S(1)}, u32[]{:S(2)}, u32[]{:S(2)}) collective-permute-start(f32[280,512]{1,0:T(8,128)S(1)} %get-tuple-element.253.refs_14_.refs_10_.refs_7_), channel_id=1, source_target_pairs={{0,8},{4,0},{8,16},{12,4},{16,24},{20,12},{24,28},{28,20},{1,9},{5... | collective-permute-start | bytes 1720328 | tf_op jit(solution)/shard_map/ppermute | solution.py:266
  164.5 15.8 %collective-permute-start.41 = (f32[264,512]{1,0:T(8,128)S(1)}, f32[264,512]{1,0:T(8,128)S(1)}, u32[]{:S(2)}, u32[]{:S(2)}) collective-permute-start(f32[264,512]{1,0:T(8,128)S(1)} %get-tuple-element.275), channel_id=1, source_target_pairs={{0,4},{4,12},{8,0},{12,20},{16,8},{20,28},{24,16},{28,24},{1,5},{5... | collective-permute-start | bytes 1622024 | tf_op jit(solution)/shard_map/ppermute | solution.py:266
  164.9 15.4 %collective-permute-start.40 = (f32[264,512]{1,0:T(8,128)S(1)}, f32[264,512]{1,0:T(8,128)S(1)}, u32[]{:S(2)}, u32[]{:S(2)}) collective-permute-start(f32[264,512]{1,0:T(8,128)S(1)} %get-tuple-element.274.refs_12_.refs_8_.refs_1_), channel_id=1, source_target_pairs={{0,8},{4,0},{8,16},{12,4},{16,24},{20,12},{24,28},{28,20},{1,9},{5... | collective-permute-start | bytes 1622024 | tf_op jit(solution)/shard_map/ppermute | solution.py:266
  181.2 18.7 %collective-permute-start.45 = (f32[264,512]{1,0:T(8,128)S(1)}, f32[264,512]{1,0:T(8,128)S(1)}, u32[]{:S(2)}, u32[]{:S(2)}) collective-permute-start(f32[264,512]{1,0:T(8,128)S(1)} %get-tuple-element.286), channel_id=1, source_target_pairs={{0,4},{4,12},{8,0},{12,20},{16,8},{20,28},{24,16},{28,24},{1,5},{5... | collective-permute-start | bytes 1622024 | tf_op jit(solution)/shard_map/ppermute | solution.py:266
  182.4 17.5 %collective-permute-start.44 = (f32[264,512]{1,0:T(8,128)S(1)}, f32[264,512]{1,0:T(8,128)S(1)}, u32[]{:S(2)}, u32[]{:S(2)}) collective-permute-start(f32[264,512]{1,0:T(8,128)S(1)} %get-tuple-element.285.refs_10_.refs_3_), channel_id=1, source_target_pairs={{0,8},{4,0},{8,16},{12,4},{16,24},{20,12},{24,28},{28,20},{1,9},{5... | collective-permute-start | bytes 1622024 | tf_op jit(solution)/shard_map/ppermute | solution.py:266
  186.3 13.6 %collective-permute-start.49 = (f32[128,1024]{1,0:T(8,128)S(1)}, f32[128,1024]{1,0:T(8,128)S(1)}, u32[]{:S(2)}, u32[]{:S(2)}) collective-permute-start(f32[128,1024]{1,0:T(8,128)S(1)} %get-tuple-element.307.refs_1_), channel_id=1, source_target_pairs={{0,1},{1,0},{2,3},{3,2},{4,5},{5,4},{6,7},{7,6},{8,9},{9,8},{10,11... | collective-permute-start | bytes 1572872 | tf_op jit(solution)/shard_map/ppermute | solution.py:245
  200.7 14.7 %collective-permute-start.51 = (f32[264,512]{1,0:T(8,128)S(1)}, f32[264,512]{1,0:T(8,128)S(1)}, u32[]{:S(2)}, u32[]{:S(2)}) collective-permute-start(f32[264,512]{1,0:T(8,128)S(1)} %get-tuple-element.296), channel_id=1, source_target_pairs={{0,4},{4,12},{8,0},{12,20},{16,8},{20,28},{24,16},{28,24},{1,5},{5... | collective-permute-start | bytes 1622024 | tf_op jit(solution)/shard_map/ppermute | solution.py:266
  200.7 14.7 %collective-permute-start.50 = (f32[264,512]{1,0:T(8,128)S(1)}, f32[264,512]{1,0:T(8,128)S(1)}, u32[]{:S(2)}, u32[]{:S(2)}) collective-permute-start(f32[264,512]{1,0:T(8,128)S(1)} %get-tuple-element.295.refs_5_), channel_id=1, source_target_pairs={{0,8},{4,0},{8,16},{12,4},{16,24},{20,12},{24,28},{28,20},{1,9},{5... | collective-permute-start | bytes 1622024 | tf_op jit(solution)/shard_map/ppermute | solution.py:266
  202.1 13.3 %collective-permute-start.53 = (f32[128,1024]{1,0:T(8,128)S(1)}, f32[128,1024]{1,0:T(8,128)S(1)}, u32[]{:S(2)}, u32[]{:S(2)}) collective-permute-start(f32[128,1024]{1,0:T(8,128)S(1)} %shard_map.121.refs_1_), channel_id=1, source_target_pairs={{0,2},{2,0},{1,3},{3,1},{4,6},{6,4},{5,7},{7,5},{8,10},{10,8},{9,1... | collective-permute-start | bytes 1572872 | tf_op jit(solution)/shard_map/ppermute | solution.py:245
  202.8 12.6 %collective-permute-start.52 = (f32[1,128]{1,0:T(1,128)S(1)}, f32[1,128]{1,0:T(1,128)S(1)}, u32[]{:S(2)}, u32[]{:S(2)}) collective-permute-start(f32[1,128]{1,0:T(1,128)S(1)} %shard_map.119.refs_7_.refs_10_), channel_id=1, source_target_pairs={{0,16},{8,24},{16,0},{24,8},{1,17},{9,25},{17,1},{25,9},{2,18},{10... | collective-permute-start | bytes 1544 | tf_op jit(solution)/shard_map/ppermute | solution.py:245
  (40 other events, 305.4 us)
where the time goes:
time: 222 us
  waiting for transfers between devices  82 us (37%)
  Pallas kernels  65.7 us (30%)
  starting transfers between devices  64.4 us (29%)
  local copies, waits for them, and re-layouts  8.33 us (4%)
    pallas_call x40, Pallas kernels, call(): pl.pallas_call(kernel, out_shape=[jax.ShapeDtypeStruct(shape, dtype) for...  65.7 us
    ppermute x23, waiting for transfers between devices, swap(): return lax.ppermute(array, axis, [(i, i ^ bit) for i in range(sizes[axis])])  34.7 us
    ppermute x23, starting transfers between devices, swap(): return lax.ppermute(array, axis, [(i, i ^ bit) for i in range(sizes[axis])])  33 us
    ppermute x8, waiting for transfers between devices, spread(): got = lax.ppermute(array, axis, [(i, (i + s) % size) for i in range(size)])  31 us
    ppermute x24, starting transfers between devices, snake(): return lax.ppermute(array, (LINE, CORE), pairs)  22.8 us
    ppermute x24, waiting for transfers between devices, snake(): return lax.ppermute(array, (LINE, CORE), pairs)  16.2 us
    ppermute x8, starting transfers between devices, spread(): got = lax.ppermute(array, axis, [(i, (i + s) % size) for i in range(size)])  8.53 us
    unnamed x34, local copies, waits for them, and re-layouts  6.66 us
  transfers between devices with their start and end apart: 55, of which 27 were waited for; matrix products, arithmetic and copies ran while one was open for 0% of the time, Pallas kernels for 19%

commit v1 on v0

--- a/solution.py
+++ b/solution.py
@@ -351,7 +351,7 @@
                 mebibytes,
             )
 
-        kept_first, away = local(0, 1, 60)
+        kept_first, away = local(0, 1, 52)
         arrived = [to_partner(away)]
 
         class Chain:
@@ -599,7 +599,7 @@
             while "squares" not in state:
                 yield 1, ()
 
-            def body(number, sums, inputs, outputs):
+            def body(number, inputs, outputs):
                 top_left, top_right, scale = scales(inputs[6][...] + inputs[7][...])
                 grad = inputs[4][...], inputs[5][...]
                 rows = pl.ds(pl.multiple_of(device(number) * own_rows, own_rows), own_rows)
@@ -611,12 +611,10 @@
                     - (5.0 * inputs[3][...] - crossed / top_left) / top_right
                 )
 
-            (state["first_part"],) = fetching(
+            (state["first_part"],) = call(
                 body,
                 [((own_rows, block), f32)],
                 numbers,
-                [],
-                shape,
                 [*crossed, *state["left_parts"], *state["block"], *state["squares"]],
             )
 
@@ -677,7 +675,7 @@
             gram = yield from over_models(gram)
             state["left_terms"] = gram
 
-            def body(number, sums, inputs, outputs):
+            def body(number, inputs, outputs):
                 gram = inputs[0][:own_rows] + inputs[1][:own_rows]
                 old = []
                 for m in range(models):
@@ -700,13 +698,11 @@
                 outputs[2][...] = gram
                 outputs[3][...] = product(grad, halves(left_grad), 1, 1).T / width
 
-            left, left_grad, gram, crossed, new = fetching(
+            left, left_grad, gram, crossed, new = call(
                 body,
                 [(rows, f32), ((own_rows, block), f32), (rows, f32), (rows, f32)]
                 + [((model_rows, own_rows), f32)],
                 numbers,
-                [],
-                shape,
                 [*gram, state["old_left"], *state["block"]],
             )
             state["left"] = left
@@ -845,7 +841,7 @@
             while len(mixed_wholes) < last or "partner_left" not in state:
                 yield 1, ()
 
-            def body(number, sums, inputs, outputs):
+            def body(number, inputs, outputs):
                 pieces = [(j, inputs[2 + j]) for j in range(last)]
                 pair = halves(jnp.concatenate([array[:piece] for _, array in pieces], axis=0))
                 for i in range(2):
@@ -855,12 +851,10 @@
                         number, i, jnp.zeros((own_rows, panel), f32), pieces
                     )
 
-            state["early"] = yield 1, fetching(
+            state["early"] = yield 1, call(
                 body,
                 [((own_rows, panel), f32)] * 4,
                 numbers,
-                [],
-                shape,
                 [state["left"], state["partner_left"], *mixed_wholes],
             )
 

time: 222 us -> 218 us (0.982)
  local copies, waits for them, and re-layouts: 8.33 us -> 2.73 us
  waiting for transfers between devices: 82 us -> 85.9 us
    unnamed x34 -> x28, local copies, waits for them, and re-layouts: 6.66 us -> 1.64 us
    ppermute x24, waiting for transfers between devices: 16.2 us -> 19.9 us  [snake(): return lax.ppermute(array, (LINE, CORE), pairs)]
  transfers between devices with their start and end apart: 55 -> 55, of which waited for: 27 -> 27; matrix products, arithmetic and copies ran while one was open for 0% -> 0% of each run, Pallas kernels for 19% -> 18%
where the time goes in v1:
time: 218 us
  waiting for transfers between devices  85.9 us (39%)
  starting transfers between devices  64.5 us (30%)
  Pallas kernels  63.5 us (29%)
  local copies, waits for them, and re-layouts  2.73 us (1%)
    pallas_call x40, Pallas kernels, call(): pl.pallas_call(kernel, out_shape=[jax.ShapeDtypeStruct(shape, dtype) for...  63.5 us
    ppermute x23, waiting for transfers between devices, swap(): return lax.ppermute(array, axis, [(i, i ^ bit) for i in range(sizes[axis])])  34.5 us
    ppermute x23, starting transfers between devices, swap(): return lax.ppermute(array, axis, [(i, i ^ bit) for i in range(sizes[axis])])  33.2 us
    ppermute x8, waiting for transfers between devices, spread(): got = lax.ppermute(array, axis, [(i, (i + s) % size) for i in range(size)])  31.5 us
    ppermute x24, starting transfers between devices, snake(): return lax.ppermute(array, (LINE, CORE), pairs)  22.8 us
    ppermute x24, waiting for transfers between devices, snake(): return lax.ppermute(array, (LINE, CORE), pairs)  19.9 us
    ppermute x8, starting transfers between devices, spread(): got = lax.ppermute(array, axis, [(i, (i + s) % size) for i in range(size)])  8.46 us
  transfers between devices with their start and end apart: 55, of which 27 were waited for; matrix products, arithmetic and copies ran while one was open for 0% of the time, Pallas kernels for 18%

profile of v1, /device:TPU:1, one launch (start us, length us, event | category | flops | bytes accessed | tf_op | source)
XLA Modules:
  0.0 217.8 jit_solution(17528337569387359134)
XLA Ops:
  0.8 3.9 %shard_map.85 = (f32[256,512]{1,0:T(8,128)S(1)}, f32[256,512]{1,0:T(8,128)S(1)}) custom-call(s32[7]{0:T(128)S(1)} %stack.39.refs_0_, bf16[1536,1024]{1,0:T(8,128)(2,1)} %refs_1_.2, bf16[1536,1024]{1,0:T(8,128)(2,1)} %refs_2_.2), custom_call_target="tpu_custom_call" | custom-call | flops 1 | bytes 1 | tf_op jit(solution)/shard_map/pallas_call | solution.py:57
  4.8 1.9 collective-permute-done.refs_2_.refs_4_.refs_6_.refs_7_
  7.4 2.4 %collective-permute-start.5 = (f32[264,512]{1,0:T(8,128)S(1)}, f32[264,512]{1,0:T(8,128)S(1)}, u32[]{:S(2)}, u32[]{:S(2)}) collective-permute-start(f32[264,512]{1,0:T(8,128)S(1)} %get-tuple-element.174), channel_id=1, source_target_pairs={{0,4},{4,12},{8,0},{12,20},{16,8},{20,28},{24,16},{28,24},{1,5},{5... | collective-permute-start | bytes 1622024 | tf_op jit(solution)/shard_map/ppermute | solution.py:266
  9.8 5.7 %shard_map.87 = (f32[768,512]{1,0:T(8,128)S(1)}, f32[256,512]{1,0:T(8,128)S(1)}, f32[256,512]{1,0:T(8,128)}, f32[256,512]{1,0:T(8,128)S(1)}) custom-call(s32[7]{0:T(128)S(1)} %stack.39.refs_0_, bf16[1536,1024]{1,0:T(8,128)(2,1)S(1)} %copy-done, bf16[1536,1024]{1,0:T(8,128)(2,1)S(1)} %copy-done.1), custom_call_target="tpu_custom_call" | custom-call | flops 1 | bytes 1 | tf_op jit(solution)/shard_map/pallas_call | solution.py:57
  16.3 4.8 %collective-permute-done.5.refs_6_.refs_13_ = f32[264,512]{1,0:T(8,128)S(1)} collective-permute-done((f32[264,512]{1,0:T(8,128)S(1)}, f32[264,512]{1,0:T(8,128)S(1)}, u32[]{:S(2)}, u32[]{:S(2)}) %collective-permute-start.5) | collective-permute-done | bytes 540704 | tf_op jit(solution)/shard_map/ppermute | solution.py:266
  21.1 1.8 collective-permute-done.4.refs_5_
  32.8 5.2 %collective-permute-done.7.refs_7_.refs_11_ = f32[264,512]{1,0:T(8,128)} collective-permute-done((f32[264,512]{1,0:T(8,128)}, f32[264,512]{1,0:T(8,128)}, u32[]{:S(2)}, u32[]{:S(2)}) %collective-permute-start.7) | collective-permute-done | bytes 540704 | tf_op jit(solution)/shard_map/ppermute | solution.py:266
  45.9 6.6 %collective-permute-done.11.refs_2_ = f32[128,512]{1,0:T(8,128)S(1)} collective-permute-done((f32[128,512]{1,0:T(8,128)S(1)}, f32[128,512]{1,0:T(8,128)S(1)}, u32[]{:S(2)}, u32[]{:S(2)}) %collective-permute-start.11) | collective-permute-done | bytes 262176 | tf_op jit(solution)/shard_map/ppermute | solution.py:245
  52.5 2.0 collective-permute-done.10.refs_8_.refs_9_.refs_10_.refs_6_
  59.9 1.9 collective-permute-start.14
  61.8 9.0 %collective-permute-done.15.refs_13_ = f32[256,512]{1,0:T(8,128)S(1)} collective-permute-done((f32[256,512]{1,0:T(8,128)S(1)}, f32[256,512]{1,0:T(8,128)S(1)}, u32[]{:S(2)}, u32[]{:S(2)}) %collective-permute-start.15) | collective-permute-done | bytes 524320 | tf_op jit(solution)/shard_map/ppermute | solution.py:492
  77.6 2.5 %collective-permute-start.19 = (f32[256,512]{1,0:T(8,128)S(1)}, f32[256,512]{1,0:T(8,128)S(1)}, u32[]{:S(2)}, u32[]{:S(2)}) collective-permute-start(f32[256,512]{1,0:T(8,128)S(1)} %get-tuple-element.202.refs_11_.refs_2_), channel_id=1, source_target_pairs={{0,4},{4,0},{1,5},{5,1},{2,6},{6,2},{3,7},{7,3},{8,12},{12,8},{9,1... | collective-permute-start | bytes 1572872 | tf_op jit(solution)/shard_map/ppermute | solution.py:245
  80.1 6.5 %collective-permute-done.18.refs_2_ = f32[256,512]{1,0:T(8,128)S(1)} collective-permute-done((f32[256,512]{1,0:T(8,128)S(1)}, f32[256,512]{1,0:T(8,128)S(1)}, u32[]{:S(2)}, u32[]{:S(2)}) %collective-permute-start.18) | collective-permute-done | bytes 524320 | tf_op jit(solution)/shard_map/ppermute | solution.py:492
  89.4 2.4 %collective-permute-start.21 = (f32[272,512]{1,0:T(8,128)S(1)}, f32[272,512]{1,0:T(8,128)S(1)}, u32[]{:S(2)}, u32[]{:S(2)}) collective-permute-start(f32[272,512]{1,0:T(8,128)S(1)} %get-tuple-element.211.refs_7_), channel_id=1, source_target_pairs={{0,8},{4,0},{8,16},{12,4},{16,24},{20,12},{24,28},{28,20},{1,9},{5... | collective-permute-start | bytes 1671176 | tf_op jit(solution)/shard_map/ppermute | solution.py:266
  94.8 2.6 %collective-permute-start.23 = (f32[256,512]{1,0:T(8,128)S(1)}, f32[256,512]{1,0:T(8,128)S(1)}, u32[]{:S(2)}, u32[]{:S(2)}) collective-permute-start(f32[256,512]{1,0:T(8,128)S(1)} %get-tuple-element.215), channel_id=1, source_target_pairs={{0,4},{4,0},{1,5},{5,1},{2,6},{6,2},{3,7},{7,3},{8,12},{12,8},{9,1... | collective-permute-start | bytes 1572872 | tf_op jit(solution)/shard_map/ppermute | solution.py:245
  99.0 4.6 %collective-permute-done.24.refs_2_ = f32[264,512]{1,0:T(8,128)S(1)} collective-permute-done((f32[264,512]{1,0:T(8,128)S(1)}, f32[264,512]{1,0:T(8,128)S(1)}, u32[]{:S(2)}, u32[]{:S(2)}) %collective-permute-start.24) | collective-permute-done | bytes 540704 | tf_op jit(solution)/shard_map/ppermute | solution.py:492
  107.8 2.9 %collective-permute-start.28 = (f32[776,512]{1,0:T(8,128)S(1)}, f32[776,512]{1,0:T(8,128)S(1)}, u32[]{:S(2)}, u32[]{:S(2)}) collective-permute-start(f32[776,512]{1,0:T(8,128)S(1)} %get-tuple-element.229), channel_id=1, source_target_pairs={{0,4},{4,0},{1,5},{5,1},{2,6},{6,2},{3,7},{7,3},{8,12},{12,8},{9,1... | collective-permute-start | bytes 4767752 | tf_op jit(solution)/shard_map/ppermute | solution.py:245
  113.9 9.2 %collective-permute-done.29.refs_2_ = f32[256,512]{1,0:T(8,128)S(1)} collective-permute-done((f32[256,512]{1,0:T(8,128)S(1)}, f32[256,512]{1,0:T(8,128)S(1)}, u32[]{:S(2)}, u32[]{:S(2)}) %collective-permute-start.29) | collective-permute-done | bytes 524320 | tf_op jit(solution)/shard_map/ppermute | solution.py:492
  128.2 3.8 %shard_map.102 = (f32[136,1024]{1,0:T(8,128)S(1)}, f32[1,1024]{1,0:T(1,128)S(1)}) custom-call(s32[7]{0:T(128)S(1)} %stack.39.refs_0_, f32[256,512]{1,0:T(8,128)S(1)} %get-tuple-element.195.refs_12_.refs_1_, f32[256,512]{1,0:T(8,128)S(1)} %get-tuple-element.202.refs_11_.refs_2_, f32[264,512]{1,0:T(8,128)S(1)} %get-tuple-element.217.refs_12_.refs_3_.refs_5_, ...), custom_call_target="tpu_custom_call" | custom-call | flops 1 | bytes 1 | tf_op jit(solution)/shard_map/pallas_call | solution.py:57
  135.1 2.3 %collective-permute-start.33 = (f32[256,512]{1,0:T(8,128)S(1)}, f32[256,512]{1,0:T(8,128)S(1)}, u32[]{:S(2)}, u32[]{:S(2)}) collective-permute-start(f32[256,512]{1,0:T(8,128)S(1)} %get-tuple-element.243), channel_id=1, source_target_pairs={{0,4},{4,0},{1,5},{5,1},{2,6},{6,2},{3,7},{7,3},{8,12},{12,8},{9,1... | collective-permute-start | bytes 1572872 | tf_op jit(solution)/shard_map/ppermute | solution.py:245
  138.9 5.3 %collective-permute-done.35.refs_2_ = f32[136,1024]{1,0:T(8,128)S(1)} collective-permute-done((f32[136,1024]{1,0:T(8,128)S(1)}, f32[136,1024]{1,0:T(8,128)S(1)}, u32[]{:S(2)}, u32[]{:S(2)}) %collective-permute-start.35) | collective-permute-done | bytes 557088 | tf_op jit(solution)/shard_map/ppermute | solution.py:245
  145.7 2.1 collective-permute-start.36
  151.5 2.3 %collective-permute-start.38 = (f32[256,512]{1,0:T(8,128)S(1)}, f32[256,512]{1,0:T(8,128)S(1)}, u32[]{:S(2)}, u32[]{:S(2)}) collective-permute-start(f32[256,512]{1,0:T(8,128)S(1)} %get-tuple-element.259), channel_id=1, source_target_pairs={{0,4},{4,0},{1,5},{5,1},{2,6},{6,2},{3,7},{7,3},{8,12},{12,8},{9,1... | collective-permute-start | bytes 1572872 | tf_op jit(solution)/shard_map/ppermute | solution.py:245
  153.9 6.0 %shard_map.107 = f32[1024,512]{1,0:T(8,128)} custom-call(s32[7]{0:T(128)S(1)} %stack.39.refs_0_, f32[1024,512]{1,0:T(8,128)S(1)} %copy-done.5, bf16[1024,1024]{1,0:T(8,128)(2,1)S(1)} %get-tuple-element.266.refs_2_.refs_4_.refs_5_, bf16[1024,1024]{1,0:T(8,128)(2,1)S(1)} %get-tuple-element.267.refs_3_.refs_5_.refs_6_, ...), custom_call_target="tpu_custom_call" | custom-call | flops 1 | bytes 1 | tf_op jit(solution)/shard_map/pallas_call | solution.py:57
  161.7 2.9 %collective-permute-start.40 = (f32[264,512]{1,0:T(8,128)S(1)}, f32[264,512]{1,0:T(8,128)S(1)}, u32[]{:S(2)}, u32[]{:S(2)}) collective-permute-start(f32[264,512]{1,0:T(8,128)S(1)} %get-tuple-element.274.refs_12_.refs_8_.refs_1_), channel_id=1, source_target_pairs={{0,8},{4,0},{8,16},{12,4},{16,24},{20,12},{24,28},{28,20},{1,9},{5... | collective-permute-start | bytes 1622024 | tf_op jit(solution)/shard_map/ppermute | solution.py:266
  164.7 2.4 %shard_map.111 = (f32[1,1664]{1,0:T(1,128)S(1)}, f32[1,1024]{1,0:T(1,128)S(1)}) custom-call(s32[7]{0:T(128)S(1)} %stack.39.refs_0_, f32[1,1024]{1,0:T(1,128)S(1)} %get-tuple-element.279.refs_1_, bf16[1024,1024]{1,0:T(8,128)(2,1)S(1)} %get-tuple-element.266.refs_2_.refs_4_.refs_5_, bf16[1024,1024]{1,0:T(8,128)(2,1)S(1)} %get-tuple-element.267.refs_3_.refs_5_.refs_6_, ...), custom_call_target="tpu_custom_call" | custom-call | flops 1 | bytes 1 | tf_op jit(solution)/shard_map/pallas_call | solution.py:57
  172.6 3.9 %shard_map.109 = (f32[128,1024]{1,0:T(8,128)S(1)}, f32[128,1024]{1,0:T(8,128)S(1)}, f32[128,1024]{1,0:T(8,128)S(1)}, f32[128,1024]{1,0:T(8,128)S(1)}, f32[256,128]{1,0:T(8,128)}) custom-call(s32[7]{0:T(128)S(1)} %stack.39.refs_0_, f32[136,1024]{1,0:T(8,128)S(1)} %shard_map.106.refs_1_.refs_6_, f32[136,1024]{1,0:T(8,128)S(1)} %collective-permute-done.39.refs_2_.refs_7_, ...), custom_call_target="tpu_custom_call" | custom-call | flops 1 | bytes 1 | tf_op jit(solution)/shard_map/pallas_call | solution.py:57
  181.0 2.0 collective-permute-start.46
  188.8 3.8 %collective-permute-done.48.refs_2_ = f32[1,128]{1,0:T(1,128)S(1)} collective-permute-done((f32[1,128]{1,0:T(1,128)S(1)}, f32[1,128]{1,0:T(1,128)S(1)}, u32[]{:S(2)}, u32[]{:S(2)}) %collective-permute-start.48) | collective-permute-done | bytes 544 | tf_op jit(solution)/shard_map/ppermute | solution.py:245
  192.6 4.0 %collective-permute-done.49.refs_2_ = f32[128,1024]{1,0:T(8,128)S(1)} collective-permute-done((f32[128,1024]{1,0:T(8,128)S(1)}, f32[128,1024]{1,0:T(8,128)S(1)}, u32[]{:S(2)}, u32[]{:S(2)}) %collective-permute-start.49) | collective-permute-done | bytes 524320 | tf_op jit(solution)/shard_map/ppermute | solution.py:245
  199.5 2.4 %collective-permute-start.52 = (f32[1,128]{1,0:T(1,128)S(1)}, f32[1,128]{1,0:T(1,128)S(1)}, u32[]{:S(2)}, u32[]{:S(2)}) collective-permute-start(f32[1,128]{1,0:T(1,128)S(1)} %shard_map.119.refs_7_.refs_10_), channel_id=1, source_target_pairs={{0,16},{8,24},{16,0},{24,8},{1,17},{9,25},{17,1},{25,9},{2,18},{10... | collective-permute-start | bytes 1544 | tf_op jit(solution)/shard_map/ppermute | solution.py:245
  203.4 8.7 %collective-permute-done.52.refs_8_.refs_11_ = f32[1,128]{1,0:T(1,128)S(1)} collective-permute-done((f32[1,128]{1,0:T(1,128)S(1)}, f32[1,128]{1,0:T(1,128)S(1)}, u32[]{:S(2)}, u32[]{:S(2)}) %collective-permute-start.52) | collective-permute-done | bytes 544 | tf_op jit(solution)/shard_map/ppermute | solution.py:245
  (151 shorter events, 88.8 us)
Async XLA Ops:
  7.4 13.7 %collective-permute-start.5 = (f32[264,512]{1,0:T(8,128)S(1)}, f32[264,512]{1,0:T(8,128)S(1)}, u32[]{:S(2)}, u32[]{:S(2)}) collective-permute-start(f32[264,512]{1,0:T(8,128)S(1)} %get-tuple-element.174), channel_id=1, source_target_pairs={{0,4},{4,12},{8,0},{12,20},{16,8},{20,28},{24,16},{28,24},{1,5},{5... | collective-permute-start | bytes 1622024 | tf_op jit(solution)/shard_map/ppermute | solution.py:266
  9.8 13.1 %collective-permute-start.4 = (f32[264,512]{1,0:T(8,128)S(1)}, f32[264,512]{1,0:T(8,128)S(1)}, u32[]{:S(2)}, u32[]{:S(2)}) collective-permute-start(f32[264,512]{1,0:T(8,128)S(1)} %get-tuple-element.173.refs_9_), channel_id=1, source_target_pairs={{0,8},{4,0},{8,16},{12,4},{16,24},{20,12},{24,28},{28,20},{1,9},{5... | collective-permute-start | bytes 1622024 | tf_op jit(solution)/shard_map/ppermute | solution.py:266
  24.6 13.4 %collective-permute-start.7 = (f32[264,512]{1,0:T(8,128)}, f32[264,512]{1,0:T(8,128)}, u32[]{:S(2)}, u32[]{:S(2)}) collective-permute-start(f32[264,512]{1,0:T(8,128)} %get-tuple-element.178), channel_id=1, source_target_pairs={{0,4},{4,12},{8,0},{12,20},{16,8},{20,28},{24,16},{28,24},{1,5},{5... | collective-permute-start | bytes 1622024 | tf_op jit(solution)/shard_map/ppermute | solution.py:266
  26.4 13.4 %collective-permute-start.6 = (f32[264,512]{1,0:T(8,128)}, f32[264,512]{1,0:T(8,128)}, u32[]{:S(2)}, u32[]{:S(2)}) collective-permute-start(f32[264,512]{1,0:T(8,128)} %get-tuple-element.177.refs_10_.refs_7_), channel_id=1, source_target_pairs={{0,8},{4,0},{8,16},{12,4},{16,24},{20,12},{24,28},{28,20},{1,9},{5... | collective-permute-start | bytes 1622024 | tf_op jit(solution)/shard_map/ppermute | solution.py:266
  26.4 13.4 %collective-permute-start.2 = (f32[256,512]{1,0:T(8,128)}, f32[256,512]{1,0:T(8,128)S(1)}, u32[]{:S(2)}, u32[]{:S(2)}) collective-permute-start(f32[256,512]{1,0:T(8,128)} %get-tuple-element.171), channel_id=1, source_target_pairs={{0,4},{4,0},{1,5},{5,1},{2,6},{6,2},{3,7},{7,3},{8,12},{12,8},{9,1... | collective-permute-start | bytes 1572872 | tf_op jit(solution)/shard_map/ppermute | solution.py:245
  41.3 13.2 %collective-permute-start.10 = (f32[264,512]{1,0:T(8,128)S(1)}, f32[264,512]{1,0:T(8,128)S(1)}, u32[]{:S(2)}, u32[]{:S(2)}) collective-permute-start(f32[264,512]{1,0:T(8,128)S(1)} %get-tuple-element.188), channel_id=1, source_target_pairs={{0,4},{4,12},{8,0},{12,20},{16,8},{20,28},{24,16},{28,24},{1,5},{5... | collective-permute-start | bytes 1622024 | tf_op jit(solution)/shard_map/ppermute | solution.py:266
  43.1 13.0 %collective-permute-start.9 = (f32[264,512]{1,0:T(8,128)S(1)}, f32[264,512]{1,0:T(8,128)S(1)}, u32[]{:S(2)}, u32[]{:S(2)}) collective-permute-start(f32[264,512]{1,0:T(8,128)S(1)} %get-tuple-element.187.refs_12_.refs_8_.refs_6_.refs_1_), channel_id=1, source_target_pairs={{0,8},{4,0},{8,16},{12,4},{16,24},{20,12},{24,28},{28,20},{1,9},{5... | collective-permute-start | bytes 1622024 | tf_op jit(solution)/shard_map/ppermute | solution.py:266
  43.1 13.0 %collective-permute-start.1 = (f32[256,512]{1,0:T(8,128)S(1)}, f32[256,512]{1,0:T(8,128)S(1)}, u32[]{:S(2)}, u32[]{:S(2)}) collective-permute-start(f32[256,512]{1,0:T(8,128)S(1)} %copy-done.12), channel_id=1, source_target_pairs={{0,4},{4,0},{1,5},{5,1},{2,6},{6,2},{3,7},{7,3},{8,12},{12,8},{9,1... | collective-permute-start | bytes 1572872 | tf_op jit(solution)/shard_map/ppermute | solution.py:245
  57.8 13.1 %collective-permute-start.13 = (f32[264,512]{1,0:T(8,128)S(1)}, f32[264,512]{1,0:T(8,128)S(1)}, u32[]{:S(2)}, u32[]{:S(2)}) collective-permute-start(f32[264,512]{1,0:T(8,128)S(1)} %get-tuple-element.194), channel_id=1, source_target_pairs={{0,4},{4,12},{8,0},{12,20},{16,8},{20,28},{24,16},{28,24},{1,5},{5... | collective-permute-start | bytes 1622024 | tf_op jit(solution)/shard_map/ppermute | solution.py:266
  58.7 13.9 %collective-permute-start.12 = (f32[264,512]{1,0:T(8,128)S(1)}, f32[264,512]{1,0:T(8,128)S(1)}, u32[]{:S(2)}, u32[]{:S(2)}) collective-permute-start(f32[264,512]{1,0:T(8,128)S(1)} %get-tuple-element.193.refs_10_.refs_7_.refs_3_), channel_id=1, source_target_pairs={{0,8},{4,0},{8,16},{12,4},{16,24},{20,12},{24,28},{28,20},{1,9},{5... | collective-permute-start | bytes 1622024 | tf_op jit(solution)/shard_map/ppermute | solution.py:266
  74.3 13.3 %collective-permute-start.17 = (f32[264,512]{1,0:T(8,128)S(1)}, f32[264,512]{1,0:T(8,128)S(1)}, u32[]{:S(2)}, u32[]{:S(2)}) collective-permute-start(f32[264,512]{1,0:T(8,128)S(1)} %get-tuple-element.200), channel_id=1, source_target_pairs={{0,4},{4,12},{8,0},{12,20},{16,8},{20,28},{24,16},{28,24},{1,5},{5... | collective-permute-start | bytes 1622024 | tf_op jit(solution)/shard_map/ppermute | solution.py:266
  74.4 13.5 %collective-permute-start.16 = (f32[264,512]{1,0:T(8,128)S(1)}, f32[264,512]{1,0:T(8,128)S(1)}, u32[]{:S(2)}, u32[]{:S(2)}) collective-permute-start(f32[264,512]{1,0:T(8,128)S(1)} %get-tuple-element.199.refs_9_.refs_5_), channel_id=1, source_target_pairs={{0,8},{4,0},{8,16},{12,4},{16,24},{20,12},{24,28},{28,20},{1,9},{5... | collective-permute-start | bytes 1622024 | tf_op jit(solution)/shard_map/ppermute | solution.py:266
  88.9 14.6 %collective-permute-start.22 = (f32[272,512]{1,0:T(8,128)S(1)}, f32[272,512]{1,0:T(8,128)S(1)}, u32[]{:S(2)}, u32[]{:S(2)}) collective-permute-start(f32[272,512]{1,0:T(8,128)S(1)} %get-tuple-element.212), channel_id=1, source_target_pairs={{0,4},{4,12},{8,0},{12,20},{16,8},{20,28},{24,16},{28,24},{1,5},{5... | collective-permute-start | bytes 1671176 | tf_op jit(solution)/shard_map/ppermute | solution.py:266
  89.4 14.1 %collective-permute-start.21 = (f32[272,512]{1,0:T(8,128)S(1)}, f32[272,512]{1,0:T(8,128)S(1)}, u32[]{:S(2)}, u32[]{:S(2)}) collective-permute-start(f32[272,512]{1,0:T(8,128)S(1)} %get-tuple-element.211.refs_7_), channel_id=1, source_target_pairs={{0,8},{4,0},{8,16},{12,4},{16,24},{20,12},{24,28},{28,20},{1,9},{5... | collective-permute-start | bytes 1671176 | tf_op jit(solution)/shard_map/ppermute | solution.py:266
  107.8 17.1 %collective-permute-start.28 = (f32[776,512]{1,0:T(8,128)S(1)}, f32[776,512]{1,0:T(8,128)S(1)}, u32[]{:S(2)}, u32[]{:S(2)}) collective-permute-start(f32[776,512]{1,0:T(8,128)S(1)} %get-tuple-element.229), channel_id=1, source_target_pairs={{0,4},{4,0},{1,5},{5,1},{2,6},{6,2},{3,7},{7,3},{8,12},{12,8},{9,1... | collective-permute-start | bytes 4767752 | tf_op jit(solution)/shard_map/ppermute | solution.py:245
  110.7 13.6 %collective-permute-start.27 = (f32[264,512]{1,0:T(8,128)S(1)}, f32[264,512]{1,0:T(8,128)S(1)}, u32[]{:S(2)}, u32[]{:S(2)}) collective-permute-start(f32[264,512]{1,0:T(8,128)S(1)} %get-tuple-element.223), channel_id=1, source_target_pairs={{0,4},{4,12},{8,0},{12,20},{16,8},{20,28},{24,16},{28,24},{1,5},{5... | collective-permute-start | bytes 1622024 | tf_op jit(solution)/shard_map/ppermute | solution.py:266
  110.9 14.0 %collective-permute-start.26 = (f32[264,512]{1,0:T(8,128)S(1)}, f32[264,512]{1,0:T(8,128)S(1)}, u32[]{:S(2)}, u32[]{:S(2)}) collective-permute-start(f32[264,512]{1,0:T(8,128)S(1)} %get-tuple-element.222.refs_11_), channel_id=1, source_target_pairs={{0,8},{4,0},{8,16},{12,4},{16,24},{20,12},{24,28},{28,20},{1,9},{5... | collective-permute-start | bytes 1622024 | tf_op jit(solution)/shard_map/ppermute | solution.py:266
  125.6 18.6 %collective-permute-start.32 = (f32[280,512]{1,0:T(8,128)S(1)}, f32[280,512]{1,0:T(8,128)S(1)}, u32[]{:S(2)}, u32[]{:S(2)}) collective-permute-start(f32[280,512]{1,0:T(8,128)S(1)} %get-tuple-element.240), channel_id=1, source_target_pairs={{0,4},{4,12},{8,0},{12,20},{16,8},{20,28},{24,16},{28,24},{1,5},{5... | collective-permute-start | bytes 1720328 | tf_op jit(solution)/shard_map/ppermute | solution.py:266
  127.3 16.9 %collective-permute-start.34 = (f32[280,512]{1,0:T(8,128)S(1)}, f32[280,512]{1,0:T(8,128)S(1)}, u32[]{:S(2)}, u32[]{:S(2)}) collective-permute-start(f32[280,512]{1,0:T(8,128)S(1)} %get-tuple-element.255.refs_1_), channel_id=1, source_target_pairs={{0,2},{2,0},{1,3},{3,1},{4,6},{6,4},{5,7},{7,5},{8,10},{10,8},{9,1... | collective-permute-start | bytes 1720328 | tf_op jit(solution)/shard_map/ppermute | solution.py:492
  127.7 16.5 %collective-permute-start.31 = (f32[280,512]{1,0:T(8,128)S(1)}, f32[280,512]{1,0:T(8,128)S(1)}, u32[]{:S(2)}, u32[]{:S(2)}) collective-permute-start(f32[280,512]{1,0:T(8,128)S(1)} %get-tuple-element.239.refs_12_.refs_9_), channel_id=1, source_target_pairs={{0,8},{4,0},{8,16},{12,4},{16,24},{20,12},{24,28},{28,20},{1,9},{5... | collective-permute-start | bytes 1720328 | tf_op jit(solution)/shard_map/ppermute | solution.py:266
  132.0 12.2 %collective-permute-start.35 = (f32[136,1024]{1,0:T(8,128)S(1)}, f32[136,1024]{1,0:T(8,128)S(1)}, u32[]{:S(2)}, u32[]{:S(2)}) collective-permute-start(f32[136,1024]{1,0:T(8,128)S(1)} %get-tuple-element.260.refs_1_), channel_id=1, source_target_pairs={{0,1},{1,0},{2,3},{3,2},{4,5},{5,4},{6,7},{7,6},{8,9},{9,8},{10,11... | collective-permute-start | bytes 1671176 | tf_op jit(solution)/shard_map/ppermute | solution.py:245
  144.9 15.7 %collective-permute-start.37 = (f32[280,512]{1,0:T(8,128)S(1)}, f32[280,512]{1,0:T(8,128)S(1)}, u32[]{:S(2)}, u32[]{:S(2)}) collective-permute-start(f32[280,512]{1,0:T(8,128)S(1)} %get-tuple-element.254), channel_id=1, source_target_pairs={{0,4},{4,12},{8,0},{12,20},{16,8},{20,28},{24,16},{28,24},{1,5},{5... | collective-permute-start | bytes 1720328 | tf_op jit(solution)/shard_map/ppermute | solution.py:266
  145.7 14.9 %collective-permute-start.36 = (f32[280,512]{1,0:T(8,128)S(1)}, f32[280,512]{1,0:T(8,128)S(1)}, u32[]{:S(2)}, u32[]{:S(2)}) collective-permute-start(f32[280,512]{1,0:T(8,128)S(1)} %get-tuple-element.253.refs_14_.refs_10_.refs_7_), channel_id=1, source_target_pairs={{0,8},{4,0},{8,16},{12,4},{16,24},{20,12},{24,28},{28,20},{1,9},{5... | collective-permute-start | bytes 1720328 | tf_op jit(solution)/shard_map/ppermute | solution.py:266
  161.7 15.3 %collective-permute-start.41 = (f32[264,512]{1,0:T(8,128)S(1)}, f32[264,512]{1,0:T(8,128)S(1)}, u32[]{:S(2)}, u32[]{:S(2)}) collective-permute-start(f32[264,512]{1,0:T(8,128)S(1)} %get-tuple-element.275), channel_id=1, source_target_pairs={{0,4},{4,12},{8,0},{12,20},{16,8},{20,28},{24,16},{28,24},{1,5},{5... | collective-permute-start | bytes 1622024 | tf_op jit(solution)/shard_map/ppermute | solution.py:266
  161.7 15.3 %collective-permute-start.40 = (f32[264,512]{1,0:T(8,128)S(1)}, f32[264,512]{1,0:T(8,128)S(1)}, u32[]{:S(2)}, u32[]{:S(2)}) collective-permute-start(f32[264,512]{1,0:T(8,128)S(1)} %get-tuple-element.274.refs_12_.refs_8_.refs_1_), channel_id=1, source_target_pairs={{0,8},{4,0},{8,16},{12,4},{16,24},{20,12},{24,28},{28,20},{1,9},{5... | collective-permute-start | bytes 1622024 | tf_op jit(solution)/shard_map/ppermute | solution.py:266
  177.9 18.7 %collective-permute-start.45 = (f32[264,512]{1,0:T(8,128)S(1)}, f32[264,512]{1,0:T(8,128)S(1)}, u32[]{:S(2)}, u32[]{:S(2)}) collective-permute-start(f32[264,512]{1,0:T(8,128)S(1)} %get-tuple-element.286), channel_id=1, source_target_pairs={{0,4},{4,12},{8,0},{12,20},{16,8},{20,28},{24,16},{28,24},{1,5},{5... | collective-permute-start | bytes 1622024 | tf_op jit(solution)/shard_map/ppermute | solution.py:266
  179.4 17.2 %collective-permute-start.44 = (f32[264,512]{1,0:T(8,128)S(1)}, f32[264,512]{1,0:T(8,128)S(1)}, u32[]{:S(2)}, u32[]{:S(2)}) collective-permute-start(f32[264,512]{1,0:T(8,128)S(1)} %get-tuple-element.285.refs_10_.refs_3_), channel_id=1, source_target_pairs={{0,8},{4,0},{8,16},{12,4},{16,24},{20,12},{24,28},{28,20},{1,9},{5... | collective-permute-start | bytes 1622024 | tf_op jit(solution)/shard_map/ppermute | solution.py:266
  183.0 13.6 %collective-permute-start.49 = (f32[128,1024]{1,0:T(8,128)S(1)}, f32[128,1024]{1,0:T(8,128)S(1)}, u32[]{:S(2)}, u32[]{:S(2)}) collective-permute-start(f32[128,1024]{1,0:T(8,128)S(1)} %get-tuple-element.307.refs_1_), channel_id=1, source_target_pairs={{0,1},{1,0},{2,3},{3,2},{4,5},{5,4},{6,7},{7,6},{8,9},{9,8},{10,11... | collective-permute-start | bytes 1572872 | tf_op jit(solution)/shard_map/ppermute | solution.py:245
  197.4 14.7 %collective-permute-start.51 = (f32[264,512]{1,0:T(8,128)S(1)}, f32[264,512]{1,0:T(8,128)S(1)}, u32[]{:S(2)}, u32[]{:S(2)}) collective-permute-start(f32[264,512]{1,0:T(8,128)S(1)} %get-tuple-element.296), channel_id=1, source_target_pairs={{0,4},{4,12},{8,0},{12,20},{16,8},{20,28},{24,16},{28,24},{1,5},{5... | collective-permute-start | bytes 1622024 | tf_op jit(solution)/shard_map/ppermute | solution.py:266
  197.5 14.7 %collective-permute-start.50 = (f32[264,512]{1,0:T(8,128)S(1)}, f32[264,512]{1,0:T(8,128)S(1)}, u32[]{:S(2)}, u32[]{:S(2)}) collective-permute-start(f32[264,512]{1,0:T(8,128)S(1)} %get-tuple-element.295.refs_5_), channel_id=1, source_target_pairs={{0,8},{4,0},{8,16},{12,4},{16,24},{20,12},{24,28},{28,20},{1,9},{5... | collective-permute-start | bytes 1622024 | tf_op jit(solution)/shard_map/ppermute | solution.py:266
  198.8 13.3 %collective-permute-start.53 = (f32[128,1024]{1,0:T(8,128)S(1)}, f32[128,1024]{1,0:T(8,128)S(1)}, u32[]{:S(2)}, u32[]{:S(2)}) collective-permute-start(f32[128,1024]{1,0:T(8,128)S(1)} %shard_map.121.refs_1_), channel_id=1, source_target_pairs={{0,2},{2,0},{1,3},{3,1},{4,6},{6,4},{5,7},{7,5},{8,10},{10,8},{9,1... | collective-permute-start | bytes 1572872 | tf_op jit(solution)/shard_map/ppermute | solution.py:245
  199.5 12.7 %collective-permute-start.52 = (f32[1,128]{1,0:T(1,128)S(1)}, f32[1,128]{1,0:T(1,128)S(1)}, u32[]{:S(2)}, u32[]{:S(2)}) collective-permute-start(f32[1,128]{1,0:T(1,128)S(1)} %shard_map.119.refs_7_.refs_10_), channel_id=1, source_target_pairs={{0,16},{8,24},{16,0},{24,8},{1,17},{9,25},{17,1},{25,9},{2,18},{10... | collective-permute-start | bytes 1544 | tf_op jit(solution)/shard_map/ppermute | solution.py:245
  (37 other events, 306.4 us)

commit v2 on v1

--- a/solution.py
+++ b/solution.py
@@ -180,11 +180,18 @@
 
                 @pl.when(number[which] == k)
                 def _():
-                    total = jnp.zeros((rows,) + shape[1:], f32)
-                    for i, (a, r) in enumerate(terms):
-                        part = inputs[a][r : r + rows]
-                        total = part if i == 0 else total + part
-                    result[at : at + rows] = total
+                    thick = min(rows, 32)
+
+                    def add(step, _):
+                        start = pl.multiple_of(step * thick, thick)
+                        total = jnp.zeros((thick,) + shape[1:], f32)
+                        for i, (a, r) in enumerate(terms):
+                            part = inputs[a][pl.ds(r + start, thick)]
+                            total = part if i == 0 else total + part
+                        result[pl.ds(at + start, thick)] = total
+                        return 0
+
+                    lax.fori_loop(0, rows // thick, add, 0)
 
         for i, (result, rows, size) in enumerate(zip(outputs, more, sizes)):
             at = shape[0]

time: 218 us -> 219 us (level)
  no operation moved by 1% of the time
where the time goes in v2:
time: 219 us
  waiting for transfers between devices  85.3 us (39%)
  starting transfers between devices  65.1 us (30%)
  Pallas kernels  64.4 us (29%)
  local copies, waits for them, and re-layouts  2.73 us (1%)
    pallas_call x40, Pallas kernels, call(): pl.pallas_call(kernel, out_shape=[jax.ShapeDtypeStruct(shape, dtype) for...  64.4 us
    ppermute x23, waiting for transfers between devices, swap(): return lax.ppermute(array, axis, [(i, i ^ bit) for i in range(sizes[axis])])  34.6 us
    ppermute x23, starting transfers between devices, swap(): return lax.ppermute(array, axis, [(i, i ^ bit) for i in range(sizes[axis])])  33.3 us
    ppermute x8, waiting for transfers between devices, spread(): got = lax.ppermute(array, axis, [(i, (i + s) % size) for i in range(size)])  31.4 us
    ppermute x24, starting transfers between devices, snake(): return lax.ppermute(array, (LINE, CORE), pairs)  23.3 us
    ppermute x24, waiting for transfers between devices, snake(): return lax.ppermute(array, (LINE, CORE), pairs)  19.4 us
    ppermute x8, starting transfers between devices, spread(): got = lax.ppermute(array, axis, [(i, (i + s) % size) for i in range(size)])  8.51 us
  transfers between devices with their start and end apart: 55, of which 27 were waited for; matrix products, arithmetic and copies ran while one was open for 0% of the time, Pallas kernels for 18%

profile of v2, /device:TPU:1, one launch (start us, length us, event | category | flops | bytes accessed | tf_op | source)
XLA Modules:
  0.0 218.7 jit_solution(13526469686719662144)
XLA Ops:
  0.8 3.9 %shard_map.85 = (f32[256,512]{1,0:T(8,128)S(1)}, f32[256,512]{1,0:T(8,128)S(1)}) custom-call(s32[7]{0:T(128)S(1)} %stack.39.refs_0_, bf16[1536,1024]{1,0:T(8,128)(2,1)} %refs_1_.2, bf16[1536,1024]{1,0:T(8,128)(2,1)} %refs_2_.2), custom_call_target="tpu_custom_call" | custom-call | flops 1 | bytes 1 | tf_op jit(solution)/shard_map/pallas_call | solution.py:57
  7.4 2.4 %collective-permute-start.5 = (f32[264,512]{1,0:T(8,128)S(1)}, f32[264,512]{1,0:T(8,128)S(1)}, u32[]{:S(2)}, u32[]{:S(2)}) collective-permute-start(f32[264,512]{1,0:T(8,128)S(1)} %get-tuple-element.174), channel_id=1, source_target_pairs={{0,4},{4,12},{8,0},{12,20},{16,8},{20,28},{24,16},{28,24},{1,5},{5... | collective-permute-start | bytes 1622024 | tf_op jit(solution)/shard_map/ppermute | solution.py:273
  9.9 5.7 %shard_map.87 = (f32[768,512]{1,0:T(8,128)S(1)}, f32[256,512]{1,0:T(8,128)S(1)}, f32[256,512]{1,0:T(8,128)}, f32[256,512]{1,0:T(8,128)S(1)}) custom-call(s32[7]{0:T(128)S(1)} %stack.39.refs_0_, bf16[1536,1024]{1,0:T(8,128)(2,1)S(1)} %copy-done, bf16[1536,1024]{1,0:T(8,128)(2,1)S(1)} %copy-done.1), custom_call_target="tpu_custom_call" | custom-call | flops 1 | bytes 1 | tf_op jit(solution)/shard_map/pallas_call | solution.py:57
  16.3 4.8 %collective-permute-done.5.refs_6_.refs_13_ = f32[264,512]{1,0:T(8,128)S(1)} collective-permute-done((f32[264,512]{1,0:T(8,128)S(1)}, f32[264,512]{1,0:T(8,128)S(1)}, u32[]{:S(2)}, u32[]{:S(2)}) %collective-permute-start.5) | collective-permute-done | bytes 540704 | tf_op jit(solution)/shard_map/ppermute | solution.py:273
  32.9 5.1 %collective-permute-done.7.refs_7_.refs_11_ = f32[264,512]{1,0:T(8,128)} collective-permute-done((f32[264,512]{1,0:T(8,128)}, f32[264,512]{1,0:T(8,128)}, u32[]{:S(2)}, u32[]{:S(2)}) %collective-permute-start.7) | collective-permute-done | bytes 540704 | tf_op jit(solution)/shard_map/ppermute | solution.py:273
  46.1 6.6 %collective-permute-done.11.refs_2_ = f32[128,512]{1,0:T(8,128)S(1)} collective-permute-done((f32[128,512]{1,0:T(8,128)S(1)}, f32[128,512]{1,0:T(8,128)S(1)}, u32[]{:S(2)}, u32[]{:S(2)}) %collective-permute-start.11) | collective-permute-done | bytes 262176 | tf_op jit(solution)/shard_map/ppermute | solution.py:252
  52.7 2.0 collective-permute-done.10.refs_8_.refs_9_.refs_10_.refs_6_
  60.3 1.9 collective-permute-start.14
  62.2 9.1 %collective-permute-done.15.refs_13_ = f32[256,512]{1,0:T(8,128)S(1)} collective-permute-done((f32[256,512]{1,0:T(8,128)S(1)}, f32[256,512]{1,0:T(8,128)S(1)}, u32[]{:S(2)}, u32[]{:S(2)}) %collective-permute-start.15) | collective-permute-done | bytes 524320 | tf_op jit(solution)/shard_map/ppermute | solution.py:499
  78.0 2.5 %collective-permute-start.19 = (f32[256,512]{1,0:T(8,128)S(1)}, f32[256,512]{1,0:T(8,128)S(1)}, u32[]{:S(2)}, u32[]{:S(2)}) collective-permute-start(f32[256,512]{1,0:T(8,128)S(1)} %get-tuple-element.202.refs_11_.refs_2_), channel_id=1, source_target_pairs={{0,4},{4,0},{1,5},{5,1},{2,6},{6,2},{3,7},{7,3},{8,12},{12,8},{9,1... | collective-permute-start | bytes 1572872 | tf_op jit(solution)/shard_map/ppermute | solution.py:252
  80.5 6.3 %collective-permute-done.18.refs_2_ = f32[256,512]{1,0:T(8,128)S(1)} collective-permute-done((f32[256,512]{1,0:T(8,128)S(1)}, f32[256,512]{1,0:T(8,128)S(1)}, u32[]{:S(2)}, u32[]{:S(2)}) %collective-permute-start.18) | collective-permute-done | bytes 524320 | tf_op jit(solution)/shard_map/ppermute | solution.py:499
  89.7 2.4 %collective-permute-start.21 = (f32[272,512]{1,0:T(8,128)S(1)}, f32[272,512]{1,0:T(8,128)S(1)}, u32[]{:S(2)}, u32[]{:S(2)}) collective-permute-start(f32[272,512]{1,0:T(8,128)S(1)} %get-tuple-element.211.refs_7_), channel_id=1, source_target_pairs={{0,8},{4,0},{8,16},{12,4},{16,24},{20,12},{24,28},{28,20},{1,9},{5... | collective-permute-start | bytes 1671176 | tf_op jit(solution)/shard_map/ppermute | solution.py:273
  95.2 2.6 %collective-permute-start.23 = (f32[256,512]{1,0:T(8,128)S(1)}, f32[256,512]{1,0:T(8,128)S(1)}, u32[]{:S(2)}, u32[]{:S(2)}) collective-permute-start(f32[256,512]{1,0:T(8,128)S(1)} %get-tuple-element.215), channel_id=1, source_target_pairs={{0,4},{4,0},{1,5},{5,1},{2,6},{6,2},{3,7},{7,3},{8,12},{12,8},{9,1... | collective-permute-start | bytes 1572872 | tf_op jit(solution)/shard_map/ppermute | solution.py:252
  99.4 4.5 %collective-permute-done.24.refs_2_ = f32[264,512]{1,0:T(8,128)S(1)} collective-permute-done((f32[264,512]{1,0:T(8,128)S(1)}, f32[264,512]{1,0:T(8,128)S(1)}, u32[]{:S(2)}, u32[]{:S(2)}) %collective-permute-start.24) | collective-permute-done | bytes 540704 | tf_op jit(solution)/shard_map/ppermute | solution.py:499
  108.1 3.0 %collective-permute-start.28 = (f32[776,512]{1,0:T(8,128)S(1)}, f32[776,512]{1,0:T(8,128)S(1)}, u32[]{:S(2)}, u32[]{:S(2)}) collective-permute-start(f32[776,512]{1,0:T(8,128)S(1)} %get-tuple-element.229), channel_id=1, source_target_pairs={{0,4},{4,0},{1,5},{5,1},{2,6},{6,2},{3,7},{7,3},{8,12},{12,8},{9,1... | collective-permute-start | bytes 4767752 | tf_op jit(solution)/shard_map/ppermute | solution.py:252
  114.3 9.2 %collective-permute-done.29.refs_2_ = f32[256,512]{1,0:T(8,128)S(1)} collective-permute-done((f32[256,512]{1,0:T(8,128)S(1)}, f32[256,512]{1,0:T(8,128)S(1)}, u32[]{:S(2)}, u32[]{:S(2)}) %collective-permute-start.29) | collective-permute-done | bytes 524320 | tf_op jit(solution)/shard_map/ppermute | solution.py:499
  126.0 1.9 collective-permute-start.32
  128.8 3.8 %shard_map.102 = (f32[136,1024]{1,0:T(8,128)S(1)}, f32[1,1024]{1,0:T(1,128)S(1)}) custom-call(s32[7]{0:T(128)S(1)} %stack.39.refs_0_, f32[256,512]{1,0:T(8,128)S(1)} %get-tuple-element.195.refs_12_.refs_1_, f32[256,512]{1,0:T(8,128)S(1)} %get-tuple-element.202.refs_11_.refs_2_, f32[264,512]{1,0:T(8,128)S(1)} %get-tuple-element.217.refs_12_.refs_3_.refs_5_, ...), custom_call_target="tpu_custom_call" | custom-call | flops 1 | bytes 1 | tf_op jit(solution)/shard_map/pallas_call | solution.py:57
  135.7 2.3 %collective-permute-start.33 = (f32[256,512]{1,0:T(8,128)S(1)}, f32[256,512]{1,0:T(8,128)S(1)}, u32[]{:S(2)}, u32[]{:S(2)}) collective-permute-start(f32[256,512]{1,0:T(8,128)S(1)} %get-tuple-element.243), channel_id=1, source_target_pairs={{0,4},{4,0},{1,5},{5,1},{2,6},{6,2},{3,7},{7,3},{8,12},{12,8},{9,1... | collective-permute-start | bytes 1572872 | tf_op jit(solution)/shard_map/ppermute | solution.py:252
  139.5 5.3 %collective-permute-done.35.refs_2_ = f32[136,1024]{1,0:T(8,128)S(1)} collective-permute-done((f32[136,1024]{1,0:T(8,128)S(1)}, f32[136,1024]{1,0:T(8,128)S(1)}, u32[]{:S(2)}, u32[]{:S(2)}) %collective-permute-start.35) | collective-permute-done | bytes 557088 | tf_op jit(solution)/shard_map/ppermute | solution.py:252
  146.5 2.0 collective-permute-start.36
  152.2 2.3 %collective-permute-start.38 = (f32[256,512]{1,0:T(8,128)S(1)}, f32[256,512]{1,0:T(8,128)S(1)}, u32[]{:S(2)}, u32[]{:S(2)}) collective-permute-start(f32[256,512]{1,0:T(8,128)S(1)} %get-tuple-element.259), channel_id=1, source_target_pairs={{0,4},{4,0},{1,5},{5,1},{2,6},{6,2},{3,7},{7,3},{8,12},{12,8},{9,1... | collective-permute-start | bytes 1572872 | tf_op jit(solution)/shard_map/ppermute | solution.py:252
  154.5 6.0 %shard_map.107 = f32[1024,512]{1,0:T(8,128)} custom-call(s32[7]{0:T(128)S(1)} %stack.39.refs_0_, f32[1024,512]{1,0:T(8,128)S(1)} %copy-done.5, bf16[1024,1024]{1,0:T(8,128)(2,1)S(1)} %get-tuple-element.266.refs_2_.refs_4_.refs_5_, bf16[1024,1024]{1,0:T(8,128)(2,1)S(1)} %get-tuple-element.267.refs_3_.refs_5_.refs_6_, ...), custom_call_target="tpu_custom_call" | custom-call | flops 1 | bytes 1 | tf_op jit(solution)/shard_map/pallas_call | solution.py:57
  162.5 2.9 %collective-permute-start.40 = (f32[264,512]{1,0:T(8,128)S(1)}, f32[264,512]{1,0:T(8,128)S(1)}, u32[]{:S(2)}, u32[]{:S(2)}) collective-permute-start(f32[264,512]{1,0:T(8,128)S(1)} %get-tuple-element.274.refs_12_.refs_8_.refs_1_), channel_id=1, source_target_pairs={{0,8},{4,0},{8,16},{12,4},{16,24},{20,12},{24,28},{28,20},{1,9},{5... | collective-permute-start | bytes 1622024 | tf_op jit(solution)/shard_map/ppermute | solution.py:273
  165.4 2.4 %shard_map.111 = (f32[1,1664]{1,0:T(1,128)S(1)}, f32[1,1024]{1,0:T(1,128)S(1)}) custom-call(s32[7]{0:T(128)S(1)} %stack.39.refs_0_, f32[1,1024]{1,0:T(1,128)S(1)} %get-tuple-element.279.refs_1_, bf16[1024,1024]{1,0:T(8,128)(2,1)S(1)} %get-tuple-element.266.refs_2_.refs_4_.refs_5_, bf16[1024,1024]{1,0:T(8,128)(2,1)S(1)} %get-tuple-element.267.refs_3_.refs_5_.refs_6_, ...), custom_call_target="tpu_custom_call" | custom-call | flops 1 | bytes 1 | tf_op jit(solution)/shard_map/pallas_call | solution.py:57
  173.3 3.9 %shard_map.109 = (f32[128,1024]{1,0:T(8,128)S(1)}, f32[128,1024]{1,0:T(8,128)S(1)}, f32[128,1024]{1,0:T(8,128)S(1)}, f32[128,1024]{1,0:T(8,128)S(1)}, f32[256,128]{1,0:T(8,128)}) custom-call(s32[7]{0:T(128)S(1)} %stack.39.refs_0_, f32[136,1024]{1,0:T(8,128)S(1)} %shard_map.106.refs_1_.refs_6_, f32[136,1024]{1,0:T(8,128)S(1)} %collective-permute-done.39.refs_2_.refs_7_, ...), custom_call_target="tpu_custom_call" | custom-call | flops 1 | bytes 1 | tf_op jit(solution)/shard_map/pallas_call | solution.py:57
  178.7 1.9 collective-permute-start.45
  181.9 2.0 collective-permute-start.46
  189.6 3.5 %collective-permute-done.48.refs_2_ = f32[1,128]{1,0:T(1,128)S(1)} collective-permute-done((f32[1,128]{1,0:T(1,128)S(1)}, f32[1,128]{1,0:T(1,128)S(1)}, u32[]{:S(2)}, u32[]{:S(2)}) %collective-permute-start.48) | collective-permute-done | bytes 544 | tf_op jit(solution)/shard_map/ppermute | solution.py:252
  193.1 4.3 %collective-permute-done.49.refs_2_ = f32[128,1024]{1,0:T(8,128)S(1)} collective-permute-done((f32[128,1024]{1,0:T(8,128)S(1)}, f32[128,1024]{1,0:T(8,128)S(1)}, u32[]{:S(2)}, u32[]{:S(2)}) %collective-permute-start.49) | collective-permute-done | bytes 524320 | tf_op jit(solution)/shard_map/ppermute | solution.py:252
  200.4 2.3 %collective-permute-start.52 = (f32[1,128]{1,0:T(1,128)S(1)}, f32[1,128]{1,0:T(1,128)S(1)}, u32[]{:S(2)}, u32[]{:S(2)}) collective-permute-start(f32[1,128]{1,0:T(1,128)S(1)} %shard_map.119.refs_7_.refs_10_), channel_id=1, source_target_pairs={{0,16},{8,24},{16,0},{24,8},{1,17},{9,25},{17,1},{25,9},{2,18},{10... | collective-permute-start | bytes 1544 | tf_op jit(solution)/shard_map/ppermute | solution.py:252
  204.3 8.8 %collective-permute-done.52.refs_8_.refs_11_ = f32[1,128]{1,0:T(1,128)S(1)} collective-permute-done((f32[1,128]{1,0:T(1,128)S(1)}, f32[1,128]{1,0:T(1,128)S(1)}, u32[]{:S(2)}, u32[]{:S(2)}) %collective-permute-start.52) | collective-permute-done | bytes 544 | tf_op jit(solution)/shard_map/ppermute | solution.py:252
  (151 shorter events, 89.9 us)
Async XLA Ops:
  7.4 13.7 %collective-permute-start.5 = (f32[264,512]{1,0:T(8,128)S(1)}, f32[264,512]{1,0:T(8,128)S(1)}, u32[]{:S(2)}, u32[]{:S(2)}) collective-permute-start(f32[264,512]{1,0:T(8,128)S(1)} %get-tuple-element.174), channel_id=1, source_target_pairs={{0,4},{4,12},{8,0},{12,20},{16,8},{20,28},{24,16},{28,24},{1,5},{5... | collective-permute-start | bytes 1622024 | tf_op jit(solution)/shard_map/ppermute | solution.py:273
  9.8 13.1 %collective-permute-start.4 = (f32[264,512]{1,0:T(8,128)S(1)}, f32[264,512]{1,0:T(8,128)S(1)}, u32[]{:S(2)}, u32[]{:S(2)}) collective-permute-start(f32[264,512]{1,0:T(8,128)S(1)} %get-tuple-element.173.refs_9_), channel_id=1, source_target_pairs={{0,8},{4,0},{8,16},{12,4},{16,24},{20,12},{24,28},{28,20},{1,9},{5... | collective-permute-start | bytes 1622024 | tf_op jit(solution)/shard_map/ppermute | solution.py:273
  24.7 13.4 %collective-permute-start.7 = (f32[264,512]{1,0:T(8,128)}, f32[264,512]{1,0:T(8,128)}, u32[]{:S(2)}, u32[]{:S(2)}) collective-permute-start(f32[264,512]{1,0:T(8,128)} %get-tuple-element.178), channel_id=1, source_target_pairs={{0,4},{4,12},{8,0},{12,20},{16,8},{20,28},{24,16},{28,24},{1,5},{5... | collective-permute-start | bytes 1622024 | tf_op jit(solution)/shard_map/ppermute | solution.py:273
  26.5 13.4 %collective-permute-start.6 = (f32[264,512]{1,0:T(8,128)}, f32[264,512]{1,0:T(8,128)}, u32[]{:S(2)}, u32[]{:S(2)}) collective-permute-start(f32[264,512]{1,0:T(8,128)} %get-tuple-element.177.refs_10_.refs_7_), channel_id=1, source_target_pairs={{0,8},{4,0},{8,16},{12,4},{16,24},{20,12},{24,28},{28,20},{1,9},{5... | collective-permute-start | bytes 1622024 | tf_op jit(solution)/shard_map/ppermute | solution.py:273
  26.5 13.4 %collective-permute-start.2 = (f32[256,512]{1,0:T(8,128)}, f32[256,512]{1,0:T(8,128)S(1)}, u32[]{:S(2)}, u32[]{:S(2)}) collective-permute-start(f32[256,512]{1,0:T(8,128)} %get-tuple-element.171), channel_id=1, source_target_pairs={{0,4},{4,0},{1,5},{5,1},{2,6},{6,2},{3,7},{7,3},{8,12},{12,8},{9,1... | collective-permute-start | bytes 1572872 | tf_op jit(solution)/shard_map/ppermute | solution.py:252
  41.4 13.2 %collective-permute-start.10 = (f32[264,512]{1,0:T(8,128)S(1)}, f32[264,512]{1,0:T(8,128)S(1)}, u32[]{:S(2)}, u32[]{:S(2)}) collective-permute-start(f32[264,512]{1,0:T(8,128)S(1)} %get-tuple-element.188), channel_id=1, source_target_pairs={{0,4},{4,12},{8,0},{12,20},{16,8},{20,28},{24,16},{28,24},{1,5},{5... | collective-permute-start | bytes 1622024 | tf_op jit(solution)/shard_map/ppermute | solution.py:273
  43.3 13.0 %collective-permute-start.9 = (f32[264,512]{1,0:T(8,128)S(1)}, f32[264,512]{1,0:T(8,128)S(1)}, u32[]{:S(2)}, u32[]{:S(2)}) collective-permute-start(f32[264,512]{1,0:T(8,128)S(1)} %get-tuple-element.187.refs_12_.refs_8_.refs_6_.refs_1_), channel_id=1, source_target_pairs={{0,8},{4,0},{8,16},{12,4},{16,24},{20,12},{24,28},{28,20},{1,9},{5... | collective-permute-start | bytes 1622024 | tf_op jit(solution)/shard_map/ppermute | solution.py:273
  43.3 13.0 %collective-permute-start.1 = (f32[256,512]{1,0:T(8,128)S(1)}, f32[256,512]{1,0:T(8,128)S(1)}, u32[]{:S(2)}, u32[]{:S(2)}) collective-permute-start(f32[256,512]{1,0:T(8,128)S(1)} %copy-done.12), channel_id=1, source_target_pairs={{0,4},{4,0},{1,5},{5,1},{2,6},{6,2},{3,7},{7,3},{8,12},{12,8},{9,1... | collective-permute-start | bytes 1572872 | tf_op jit(solution)/shard_map/ppermute | solution.py:252
  58.0 13.3 %collective-permute-start.13 = (f32[264,512]{1,0:T(8,128)S(1)}, f32[264,512]{1,0:T(8,128)S(1)}, u32[]{:S(2)}, u32[]{:S(2)}) collective-permute-start(f32[264,512]{1,0:T(8,128)S(1)} %get-tuple-element.194), channel_id=1, source_target_pairs={{0,4},{4,12},{8,0},{12,20},{16,8},{20,28},{24,16},{28,24},{1,5},{5... | collective-permute-start | bytes 1622024 | tf_op jit(solution)/shard_map/ppermute | solution.py:273
  59.0 13.9 %collective-permute-start.12 = (f32[264,512]{1,0:T(8,128)S(1)}, f32[264,512]{1,0:T(8,128)S(1)}, u32[]{:S(2)}, u32[]{:S(2)}) collective-permute-start(f32[264,512]{1,0:T(8,128)S(1)} %get-tuple-element.193.refs_10_.refs_7_.refs_3_), channel_id=1, source_target_pairs={{0,8},{4,0},{8,16},{12,4},{16,24},{20,12},{24,28},{28,20},{1,9},{5... | collective-permute-start | bytes 1622024 | tf_op jit(solution)/shard_map/ppermute | solution.py:273
  74.6 13.3 %collective-permute-start.17 = (f32[264,512]{1,0:T(8,128)S(1)}, f32[264,512]{1,0:T(8,128)S(1)}, u32[]{:S(2)}, u32[]{:S(2)}) collective-permute-start(f32[264,512]{1,0:T(8,128)S(1)} %get-tuple-element.200), channel_id=1, source_target_pairs={{0,4},{4,12},{8,0},{12,20},{16,8},{20,28},{24,16},{28,24},{1,5},{5... | collective-permute-start | bytes 1622024 | tf_op jit(solution)/shard_map/ppermute | solution.py:273
  74.7 13.5 %collective-permute-start.16 = (f32[264,512]{1,0:T(8,128)S(1)}, f32[264,512]{1,0:T(8,128)S(1)}, u32[]{:S(2)}, u32[]{:S(2)}) collective-permute-start(f32[264,512]{1,0:T(8,128)S(1)} %get-tuple-element.199.refs_9_.refs_5_), channel_id=1, source_target_pairs={{0,8},{4,0},{8,16},{12,4},{16,24},{20,12},{24,28},{28,20},{1,9},{5... | collective-permute-start | bytes 1622024 | tf_op jit(solution)/shard_map/ppermute | solution.py:273
  89.2 14.7 %collective-permute-start.22 = (f32[272,512]{1,0:T(8,128)S(1)}, f32[272,512]{1,0:T(8,128)S(1)}, u32[]{:S(2)}, u32[]{:S(2)}) collective-permute-start(f32[272,512]{1,0:T(8,128)S(1)} %get-tuple-element.212), channel_id=1, source_target_pairs={{0,4},{4,12},{8,0},{12,20},{16,8},{20,28},{24,16},{28,24},{1,5},{5... | collective-permute-start | bytes 1671176 | tf_op jit(solution)/shard_map/ppermute | solution.py:273
  89.7 14.2 %collective-permute-start.21 = (f32[272,512]{1,0:T(8,128)S(1)}, f32[272,512]{1,0:T(8,128)S(1)}, u32[]{:S(2)}, u32[]{:S(2)}) collective-permute-start(f32[272,512]{1,0:T(8,128)S(1)} %get-tuple-element.211.refs_7_), channel_id=1, source_target_pairs={{0,8},{4,0},{8,16},{12,4},{16,24},{20,12},{24,28},{28,20},{1,9},{5... | collective-permute-start | bytes 1671176 | tf_op jit(solution)/shard_map/ppermute | solution.py:273
  108.1 16.9 %collective-permute-start.28 = (f32[776,512]{1,0:T(8,128)S(1)}, f32[776,512]{1,0:T(8,128)S(1)}, u32[]{:S(2)}, u32[]{:S(2)}) collective-permute-start(f32[776,512]{1,0:T(8,128)S(1)} %get-tuple-element.229), channel_id=1, source_target_pairs={{0,4},{4,0},{1,5},{5,1},{2,6},{6,2},{3,7},{7,3},{8,12},{12,8},{9,1... | collective-permute-start | bytes 4767752 | tf_op jit(solution)/shard_map/ppermute | solution.py:252
  111.1 13.5 %collective-permute-start.27 = (f32[264,512]{1,0:T(8,128)S(1)}, f32[264,512]{1,0:T(8,128)S(1)}, u32[]{:S(2)}, u32[]{:S(2)}) collective-permute-start(f32[264,512]{1,0:T(8,128)S(1)} %get-tuple-element.223), channel_id=1, source_target_pairs={{0,4},{4,12},{8,0},{12,20},{16,8},{20,28},{24,16},{28,24},{1,5},{5... | collective-permute-start | bytes 1622024 | tf_op jit(solution)/shard_map/ppermute | solution.py:273
  111.1 13.9 %collective-permute-start.26 = (f32[264,512]{1,0:T(8,128)S(1)}, f32[264,512]{1,0:T(8,128)S(1)}, u32[]{:S(2)}, u32[]{:S(2)}) collective-permute-start(f32[264,512]{1,0:T(8,128)S(1)} %get-tuple-element.222.refs_11_), channel_id=1, source_target_pairs={{0,8},{4,0},{8,16},{12,4},{16,24},{20,12},{24,28},{28,20},{1,9},{5... | collective-permute-start | bytes 1622024 | tf_op jit(solution)/shard_map/ppermute | solution.py:273
  126.0 18.8 %collective-permute-start.32 = (f32[280,512]{1,0:T(8,128)S(1)}, f32[280,512]{1,0:T(8,128)S(1)}, u32[]{:S(2)}, u32[]{:S(2)}) collective-permute-start(f32[280,512]{1,0:T(8,128)S(1)} %get-tuple-element.240), channel_id=1, source_target_pairs={{0,4},{4,12},{8,0},{12,20},{16,8},{20,28},{24,16},{28,24},{1,5},{5... | collective-permute-start | bytes 1720328 | tf_op jit(solution)/shard_map/ppermute | solution.py:273
  127.9 16.9 %collective-permute-start.34 = (f32[280,512]{1,0:T(8,128)S(1)}, f32[280,512]{1,0:T(8,128)S(1)}, u32[]{:S(2)}, u32[]{:S(2)}) collective-permute-start(f32[280,512]{1,0:T(8,128)S(1)} %get-tuple-element.255.refs_1_), channel_id=1, source_target_pairs={{0,2},{2,0},{1,3},{3,1},{4,6},{6,4},{5,7},{7,5},{8,10},{10,8},{9,1... | collective-permute-start | bytes 1720328 | tf_op jit(solution)/shard_map/ppermute | solution.py:499
  128.3 16.6 %collective-permute-start.31 = (f32[280,512]{1,0:T(8,128)S(1)}, f32[280,512]{1,0:T(8,128)S(1)}, u32[]{:S(2)}, u32[]{:S(2)}) collective-permute-start(f32[280,512]{1,0:T(8,128)S(1)} %get-tuple-element.239.refs_12_.refs_9_), channel_id=1, source_target_pairs={{0,8},{4,0},{8,16},{12,4},{16,24},{20,12},{24,28},{28,20},{1,9},{5... | collective-permute-start | bytes 1720328 | tf_op jit(solution)/shard_map/ppermute | solution.py:273
  132.6 12.2 %collective-permute-start.35 = (f32[136,1024]{1,0:T(8,128)S(1)}, f32[136,1024]{1,0:T(8,128)S(1)}, u32[]{:S(2)}, u32[]{:S(2)}) collective-permute-start(f32[136,1024]{1,0:T(8,128)S(1)} %get-tuple-element.260.refs_1_), channel_id=1, source_target_pairs={{0,1},{1,0},{2,3},{3,2},{4,5},{5,4},{6,7},{7,6},{8,9},{9,8},{10,11... | collective-permute-start | bytes 1671176 | tf_op jit(solution)/shard_map/ppermute | solution.py:252
  145.6 15.7 %collective-permute-start.37 = (f32[280,512]{1,0:T(8,128)S(1)}, f32[280,512]{1,0:T(8,128)S(1)}, u32[]{:S(2)}, u32[]{:S(2)}) collective-permute-start(f32[280,512]{1,0:T(8,128)S(1)} %get-tuple-element.254), channel_id=1, source_target_pairs={{0,4},{4,12},{8,0},{12,20},{16,8},{20,28},{24,16},{28,24},{1,5},{5... | collective-permute-start | bytes 1720328 | tf_op jit(solution)/shard_map/ppermute | solution.py:273
  146.5 14.8 %collective-permute-start.36 = (f32[280,512]{1,0:T(8,128)S(1)}, f32[280,512]{1,0:T(8,128)S(1)}, u32[]{:S(2)}, u32[]{:S(2)}) collective-permute-start(f32[280,512]{1,0:T(8,128)S(1)} %get-tuple-element.253.refs_14_.refs_10_.refs_7_), channel_id=1, source_target_pairs={{0,8},{4,0},{8,16},{12,4},{16,24},{20,12},{24,28},{28,20},{1,9},{5... | collective-permute-start | bytes 1720328 | tf_op jit(solution)/shard_map/ppermute | solution.py:273
  162.5 15.3 %collective-permute-start.41 = (f32[264,512]{1,0:T(8,128)S(1)}, f32[264,512]{1,0:T(8,128)S(1)}, u32[]{:S(2)}, u32[]{:S(2)}) collective-permute-start(f32[264,512]{1,0:T(8,128)S(1)} %get-tuple-element.275), channel_id=1, source_target_pairs={{0,4},{4,12},{8,0},{12,20},{16,8},{20,28},{24,16},{28,24},{1,5},{5... | collective-permute-start | bytes 1622024 | tf_op jit(solution)/shard_map/ppermute | solution.py:273
  162.5 15.3 %collective-permute-start.40 = (f32[264,512]{1,0:T(8,128)S(1)}, f32[264,512]{1,0:T(8,128)S(1)}, u32[]{:S(2)}, u32[]{:S(2)}) collective-permute-start(f32[264,512]{1,0:T(8,128)S(1)} %get-tuple-element.274.refs_12_.refs_8_.refs_1_), channel_id=1, source_target_pairs={{0,8},{4,0},{8,16},{12,4},{16,24},{20,12},{24,28},{28,20},{1,9},{5... | collective-permute-start | bytes 1622024 | tf_op jit(solution)/shard_map/ppermute | solution.py:273
  178.7 18.7 %collective-permute-start.45 = (f32[264,512]{1,0:T(8,128)S(1)}, f32[264,512]{1,0:T(8,128)S(1)}, u32[]{:S(2)}, u32[]{:S(2)}) collective-permute-start(f32[264,512]{1,0:T(8,128)S(1)} %get-tuple-element.286), channel_id=1, source_target_pairs={{0,4},{4,12},{8,0},{12,20},{16,8},{20,28},{24,16},{28,24},{1,5},{5... | collective-permute-start | bytes 1622024 | tf_op jit(solution)/shard_map/ppermute | solution.py:273
  180.6 16.8 %collective-permute-start.44 = (f32[264,512]{1,0:T(8,128)S(1)}, f32[264,512]{1,0:T(8,128)S(1)}, u32[]{:S(2)}, u32[]{:S(2)}) collective-permute-start(f32[264,512]{1,0:T(8,128)S(1)} %get-tuple-element.285.refs_10_.refs_3_), channel_id=1, source_target_pairs={{0,8},{4,0},{8,16},{12,4},{16,24},{20,12},{24,28},{28,20},{1,9},{5... | collective-permute-start | bytes 1622024 | tf_op jit(solution)/shard_map/ppermute | solution.py:273
  183.9 13.6 %collective-permute-start.49 = (f32[128,1024]{1,0:T(8,128)S(1)}, f32[128,1024]{1,0:T(8,128)S(1)}, u32[]{:S(2)}, u32[]{:S(2)}) collective-permute-start(f32[128,1024]{1,0:T(8,128)S(1)} %get-tuple-element.307.refs_1_), channel_id=1, source_target_pairs={{0,1},{1,0},{2,3},{3,2},{4,5},{5,4},{6,7},{7,6},{8,9},{9,8},{10,11... | collective-permute-start | bytes 1572872 | tf_op jit(solution)/shard_map/ppermute | solution.py:252
  198.3 14.7 %collective-permute-start.51 = (f32[264,512]{1,0:T(8,128)S(1)}, f32[264,512]{1,0:T(8,128)S(1)}, u32[]{:S(2)}, u32[]{:S(2)}) collective-permute-start(f32[264,512]{1,0:T(8,128)S(1)} %get-tuple-element.296), channel_id=1, source_target_pairs={{0,4},{4,12},{8,0},{12,20},{16,8},{20,28},{24,16},{28,24},{1,5},{5... | collective-permute-start | bytes 1622024 | tf_op jit(solution)/shard_map/ppermute | solution.py:273
  198.4 14.7 %collective-permute-start.50 = (f32[264,512]{1,0:T(8,128)S(1)}, f32[264,512]{1,0:T(8,128)S(1)}, u32[]{:S(2)}, u32[]{:S(2)}) collective-permute-start(f32[264,512]{1,0:T(8,128)S(1)} %get-tuple-element.295.refs_5_), channel_id=1, source_target_pairs={{0,8},{4,0},{8,16},{12,4},{16,24},{20,12},{24,28},{28,20},{1,9},{5... | collective-permute-start | bytes 1622024 | tf_op jit(solution)/shard_map/ppermute | solution.py:273
  199.8 13.3 %collective-permute-start.53 = (f32[128,1024]{1,0:T(8,128)S(1)}, f32[128,1024]{1,0:T(8,128)S(1)}, u32[]{:S(2)}, u32[]{:S(2)}) collective-permute-start(f32[128,1024]{1,0:T(8,128)S(1)} %shard_map.121.refs_1_), channel_id=1, source_target_pairs={{0,2},{2,0},{1,3},{3,1},{4,6},{6,4},{5,7},{7,5},{8,10},{10,8},{9,1... | collective-permute-start | bytes 1572872 | tf_op jit(solution)/shard_map/ppermute | solution.py:252
  200.4 12.7 %collective-permute-start.52 = (f32[1,128]{1,0:T(1,128)S(1)}, f32[1,128]{1,0:T(1,128)S(1)}, u32[]{:S(2)}, u32[]{:S(2)}) collective-permute-start(f32[1,128]{1,0:T(1,128)S(1)} %shard_map.119.refs_7_.refs_10_), channel_id=1, source_target_pairs={{0,16},{8,24},{16,0},{24,8},{1,17},{9,25},{17,1},{25,9},{2,18},{10... | collective-permute-start | bytes 1544 | tf_op jit(solution)/shard_map/ppermute | solution.py:252
  (37 other events, 306.1 us)

commit v3 on v1

--- a/solution.py
+++ b/solution.py
@@ -43,7 +43,7 @@
     return lax.optimization_barrier(tuple(values))
 
 
-def call(body, outputs, numbers, arrays, space=pltpu.VMEM, scratch=(), mebibytes=24):
+def call(body, outputs, numbers, arrays, space=pltpu.VMEM, scratch=(), mebibytes=20):
     inputs, results = len(arrays), len(outputs)
 
     def kernel(*refs):
@@ -889,7 +889,7 @@
                 )
                 windows.add(old_factors())
                 windows.add(old_left())
-                kept, *away = local(1, count, 40)
+                kept, *away = local(1, count, 28)
                 kept_rest.append(kept)
                 arrived += [to_partner(a) for a in away]
             current.send(*results[:2])

time: 218 us -> 218 us (level)
  no operation moved by 1% of the time
where the time goes in v3:
time: 218 us; the launch traced here: 217 us
  waiting for transfers between devices  84.6 us (39%)
  starting transfers between devices  64.7 us (30%)
  Pallas kernels  63.5 us (29%)
  local copies, waits for them, and re-layouts  3.53 us (2%)
    pallas_call x40, Pallas kernels, call(): pl.pallas_call(kernel, out_shape=[jax.ShapeDtypeStruct(shape, dtype) for...  63.5 us
    ppermute x23, waiting for transfers between devices, swap(): return lax.ppermute(array, axis, [(i, i ^ bit) for i in range(sizes[axis])])  34.3 us
    ppermute x23, starting transfers between devices, swap(): return lax.ppermute(array, axis, [(i, i ^ bit) for i in range(sizes[axis])])  33.3 us
    ppermute x8, waiting for transfers between devices, spread(): got = lax.ppermute(array, axis, [(i, (i + s) % size) for i in range(size)])  31.1 us
    ppermute x24, starting transfers between devices, snake(): return lax.ppermute(array, (LINE, CORE), pairs)  22.9 us
    ppermute x24, waiting for transfers between devices, snake(): return lax.ppermute(array, (LINE, CORE), pairs)  19.2 us
    ppermute x8, starting transfers between devices, spread(): got = lax.ppermute(array, axis, [(i, (i + s) % size) for i in range(size)])  8.51 us
  transfers between devices with their start and end apart: 55, of which 27 were waited for; matrix products, arithmetic and copies ran while one was open for 0% of the time, Pallas kernels for 18%

profile of v3, /device:TPU:1, one launch (start us, length us, event | category | flops | bytes accessed | tf_op | source)
XLA Modules:
  0.0 217.5 jit_solution(18155825163815423451)
XLA Ops:
  0.8 3.9 %shard_map.85 = (f32[256,512]{1,0:T(8,128)S(1)}, f32[256,512]{1,0:T(8,128)S(1)}) custom-call(s32[7]{0:T(128)S(1)} %stack.39.refs_0_, bf16[1536,1024]{1,0:T(8,128)(2,1)} %refs_1_.2, bf16[1536,1024]{1,0:T(8,128)(2,1)} %refs_2_.2), custom_call_target="tpu_custom_call" | custom-call | flops 1 | bytes 1 | tf_op jit(solution)/shard_map/pallas_call | solution.py:57
  7.4 2.4 %collective-permute-start.5 = (f32[264,512]{1,0:T(8,128)S(1)}, f32[264,512]{1,0:T(8,128)S(1)}, u32[]{:S(2)}, u32[]{:S(2)}) collective-permute-start(f32[264,512]{1,0:T(8,128)S(1)} %get-tuple-element.174), channel_id=1, source_target_pairs={{0,4},{4,12},{8,0},{12,20},{16,8},{20,28},{24,16},{28,24},{1,5},{5... | collective-permute-start | bytes 1622024 | tf_op jit(solution)/shard_map/ppermute | solution.py:266
  9.8 5.7 %shard_map.87 = (f32[768,512]{1,0:T(8,128)S(1)}, f32[256,512]{1,0:T(8,128)S(1)}, f32[256,512]{1,0:T(8,128)}, f32[256,512]{1,0:T(8,128)S(1)}) custom-call(s32[7]{0:T(128)S(1)} %stack.39.refs_0_, bf16[1536,1024]{1,0:T(8,128)(2,1)S(1)} %copy-done, bf16[1536,1024]{1,0:T(8,128)(2,1)S(1)} %copy-done.1), custom_call_target="tpu_custom_call" | custom-call | flops 1 | bytes 1 | tf_op jit(solution)/shard_map/pallas_call | solution.py:57
  17.0 4.0 %collective-permute-done.5.refs_6_.refs_13_ = f32[264,512]{1,0:T(8,128)S(1)} collective-permute-done((f32[264,512]{1,0:T(8,128)S(1)}, f32[264,512]{1,0:T(8,128)S(1)}, u32[]{:S(2)}, u32[]{:S(2)}) %collective-permute-start.5) | collective-permute-done | bytes 540704 | tf_op jit(solution)/shard_map/ppermute | solution.py:266
  32.8 5.2 %collective-permute-done.7.refs_7_.refs_11_ = f32[264,512]{1,0:T(8,128)} collective-permute-done((f32[264,512]{1,0:T(8,128)}, f32[264,512]{1,0:T(8,128)}, u32[]{:S(2)}, u32[]{:S(2)}) %collective-permute-start.7) | collective-permute-done | bytes 540704 | tf_op jit(solution)/shard_map/ppermute | solution.py:266
  45.9 6.5 %collective-permute-done.11.refs_2_ = f32[128,512]{1,0:T(8,128)S(1)} collective-permute-done((f32[128,512]{1,0:T(8,128)S(1)}, f32[128,512]{1,0:T(8,128)S(1)}, u32[]{:S(2)}, u32[]{:S(2)}) %collective-permute-start.11) | collective-permute-done | bytes 262176 | tf_op jit(solution)/shard_map/ppermute | solution.py:245
  52.4 2.1 collective-permute-done.10.refs_8_.refs_9_.refs_10_.refs_6_
  59.9 1.9 collective-permute-start.14
  61.8 8.8 %collective-permute-done.15.refs_13_ = f32[256,512]{1,0:T(8,128)S(1)} collective-permute-done((f32[256,512]{1,0:T(8,128)S(1)}, f32[256,512]{1,0:T(8,128)S(1)}, u32[]{:S(2)}, u32[]{:S(2)}) %collective-permute-start.15) | collective-permute-done | bytes 524320 | tf_op jit(solution)/shard_map/ppermute | solution.py:492
  70.6 1.9 collective-permute-done.12.refs_3_
  77.4 2.6 %collective-permute-start.19 = (f32[256,512]{1,0:T(8,128)S(1)}, f32[256,512]{1,0:T(8,128)S(1)}, u32[]{:S(2)}, u32[]{:S(2)}) collective-permute-start(f32[256,512]{1,0:T(8,128)S(1)} %get-tuple-element.202.refs_11_.refs_2_), channel_id=1, source_target_pairs={{0,4},{4,0},{1,5},{5,1},{2,6},{6,2},{3,7},{7,3},{8,12},{12,8},{9,1... | collective-permute-start | bytes 1572872 | tf_op jit(solution)/shard_map/ppermute | solution.py:245
  79.9 6.3 %collective-permute-done.18.refs_2_ = f32[256,512]{1,0:T(8,128)S(1)} collective-permute-done((f32[256,512]{1,0:T(8,128)S(1)}, f32[256,512]{1,0:T(8,128)S(1)}, u32[]{:S(2)}, u32[]{:S(2)}) %collective-permute-start.18) | collective-permute-done | bytes 524320 | tf_op jit(solution)/shard_map/ppermute | solution.py:492
  89.0 2.6 %collective-permute-start.21 = (f32[272,512]{1,0:T(8,128)S(1)}, f32[272,512]{1,0:T(8,128)S(1)}, u32[]{:S(2)}, u32[]{:S(2)}) collective-permute-start(f32[272,512]{1,0:T(8,128)S(1)} %get-tuple-element.211.refs_7_), channel_id=1, source_target_pairs={{0,8},{4,0},{8,16},{12,4},{16,24},{20,12},{24,28},{28,20},{1,9},{5... | collective-permute-start | bytes 1671176 | tf_op jit(solution)/shard_map/ppermute | solution.py:266
  94.6 2.6 %collective-permute-start.23 = (f32[256,512]{1,0:T(8,128)S(1)}, f32[256,512]{1,0:T(8,128)S(1)}, u32[]{:S(2)}, u32[]{:S(2)}) collective-permute-start(f32[256,512]{1,0:T(8,128)S(1)} %get-tuple-element.215), channel_id=1, source_target_pairs={{0,4},{4,0},{1,5},{5,1},{2,6},{6,2},{3,7},{7,3},{8,12},{12,8},{9,1... | collective-permute-start | bytes 1572872 | tf_op jit(solution)/shard_map/ppermute | solution.py:245
  98.7 4.6 %collective-permute-done.24.refs_2_ = f32[264,512]{1,0:T(8,128)S(1)} collective-permute-done((f32[264,512]{1,0:T(8,128)S(1)}, f32[264,512]{1,0:T(8,128)S(1)}, u32[]{:S(2)}, u32[]{:S(2)}) %collective-permute-start.24) | collective-permute-done | bytes 540704 | tf_op jit(solution)/shard_map/ppermute | solution.py:492
  107.5 3.0 %collective-permute-start.28 = (f32[776,512]{1,0:T(8,128)S(1)}, f32[776,512]{1,0:T(8,128)S(1)}, u32[]{:S(2)}, u32[]{:S(2)}) collective-permute-start(f32[776,512]{1,0:T(8,128)S(1)} %get-tuple-element.229), channel_id=1, source_target_pairs={{0,4},{4,0},{1,5},{5,1},{2,6},{6,2},{3,7},{7,3},{8,12},{12,8},{9,1... | collective-permute-start | bytes 4767752 | tf_op jit(solution)/shard_map/ppermute | solution.py:245
  113.7 9.2 %collective-permute-done.29.refs_2_ = f32[256,512]{1,0:T(8,128)S(1)} collective-permute-done((f32[256,512]{1,0:T(8,128)S(1)}, f32[256,512]{1,0:T(8,128)S(1)}, u32[]{:S(2)}, u32[]{:S(2)}) %collective-permute-start.29) | collective-permute-done | bytes 524320 | tf_op jit(solution)/shard_map/ppermute | solution.py:492
  125.1 1.9 collective-permute-start.32
  128.0 3.8 %shard_map.102 = (f32[136,1024]{1,0:T(8,128)S(1)}, f32[1,1024]{1,0:T(1,128)S(1)}) custom-call(s32[7]{0:T(128)S(1)} %stack.39.refs_0_, f32[256,512]{1,0:T(8,128)S(1)} %get-tuple-element.195.refs_12_.refs_1_, f32[256,512]{1,0:T(8,128)S(1)} %get-tuple-element.202.refs_11_.refs_2_, f32[264,512]{1,0:T(8,128)S(1)} %get-tuple-element.217.refs_12_.refs_3_.refs_5_, ...), custom_call_target="tpu_custom_call" | custom-call | flops 1 | bytes 1 | tf_op jit(solution)/shard_map/pallas_call | solution.py:57
  134.8 2.3 %collective-permute-start.33 = (f32[256,512]{1,0:T(8,128)S(1)}, f32[256,512]{1,0:T(8,128)S(1)}, u32[]{:S(2)}, u32[]{:S(2)}) collective-permute-start(f32[256,512]{1,0:T(8,128)S(1)} %get-tuple-element.243), channel_id=1, source_target_pairs={{0,4},{4,0},{1,5},{5,1},{2,6},{6,2},{3,7},{7,3},{8,12},{12,8},{9,1... | collective-permute-start | bytes 1572872 | tf_op jit(solution)/shard_map/ppermute | solution.py:245
  138.6 5.3 %collective-permute-done.35.refs_2_ = f32[136,1024]{1,0:T(8,128)S(1)} collective-permute-done((f32[136,1024]{1,0:T(8,128)S(1)}, f32[136,1024]{1,0:T(8,128)S(1)}, u32[]{:S(2)}, u32[]{:S(2)}) %collective-permute-start.35) | collective-permute-done | bytes 557088 | tf_op jit(solution)/shard_map/ppermute | solution.py:245
  145.6 2.0 collective-permute-start.36
  151.3 2.3 %collective-permute-start.38 = (f32[256,512]{1,0:T(8,128)S(1)}, f32[256,512]{1,0:T(8,128)S(1)}, u32[]{:S(2)}, u32[]{:S(2)}) collective-permute-start(f32[256,512]{1,0:T(8,128)S(1)} %get-tuple-element.259), channel_id=1, source_target_pairs={{0,4},{4,0},{1,5},{5,1},{2,6},{6,2},{3,7},{7,3},{8,12},{12,8},{9,1... | collective-permute-start | bytes 1572872 | tf_op jit(solution)/shard_map/ppermute | solution.py:245
  153.6 6.0 %shard_map.107 = f32[1024,512]{1,0:T(8,128)} custom-call(s32[7]{0:T(128)S(1)} %stack.39.refs_0_, f32[1024,512]{1,0:T(8,128)S(1)} %copy-done.5, bf16[1024,1024]{1,0:T(8,128)(2,1)S(1)} %get-tuple-element.266.refs_2_.refs_4_.refs_5_, bf16[1024,1024]{1,0:T(8,128)(2,1)S(1)} %get-tuple-element.267.refs_3_.refs_5_.refs_6_, ...), custom_call_target="tpu_custom_call" | custom-call | flops 1 | bytes 1 | tf_op jit(solution)/shard_map/pallas_call | solution.py:57
  161.5 2.9 %collective-permute-start.40 = (f32[264,512]{1,0:T(8,128)S(1)}, f32[264,512]{1,0:T(8,128)S(1)}, u32[]{:S(2)}, u32[]{:S(2)}) collective-permute-start(f32[264,512]{1,0:T(8,128)S(1)} %get-tuple-element.274.refs_12_.refs_8_.refs_1_), channel_id=1, source_target_pairs={{0,8},{4,0},{8,16},{12,4},{16,24},{20,12},{24,28},{28,20},{1,9},{5... | collective-permute-start | bytes 1622024 | tf_op jit(solution)/shard_map/ppermute | solution.py:266
  164.4 2.4 %shard_map.111 = (f32[1,1664]{1,0:T(1,128)S(1)}, f32[1,1024]{1,0:T(1,128)S(1)}) custom-call(s32[7]{0:T(128)S(1)} %stack.39.refs_0_, f32[1,1024]{1,0:T(1,128)S(1)} %get-tuple-element.279.refs_1_, bf16[1024,1024]{1,0:T(8,128)(2,1)S(1)} %get-tuple-element.266.refs_2_.refs_4_.refs_5_, bf16[1024,1024]{1,0:T(8,128)(2,1)S(1)} %get-tuple-element.267.refs_3_.refs_5_.refs_6_, ...), custom_call_target="tpu_custom_call" | custom-call | flops 1 | bytes 1 | tf_op jit(solution)/shard_map/pallas_call | solution.py:57
  172.3 3.9 %shard_map.109 = (f32[128,1024]{1,0:T(8,128)S(1)}, f32[128,1024]{1,0:T(8,128)S(1)}, f32[128,1024]{1,0:T(8,128)S(1)}, f32[128,1024]{1,0:T(8,128)S(1)}, f32[256,128]{1,0:T(8,128)}) custom-call(s32[7]{0:T(128)S(1)} %stack.39.refs_0_, f32[136,1024]{1,0:T(8,128)S(1)} %shard_map.106.refs_1_.refs_6_, f32[136,1024]{1,0:T(8,128)S(1)} %collective-permute-done.39.refs_2_.refs_7_, ...), custom_call_target="tpu_custom_call" | custom-call | flops 1 | bytes 1 | tf_op jit(solution)/shard_map/pallas_call | solution.py:57
  180.8 2.0 collective-permute-start.46
  188.6 3.7 %collective-permute-done.48.refs_2_ = f32[1,128]{1,0:T(1,128)S(1)} collective-permute-done((f32[1,128]{1,0:T(1,128)S(1)}, f32[1,128]{1,0:T(1,128)S(1)}, u32[]{:S(2)}, u32[]{:S(2)}) %collective-permute-start.48) | collective-permute-done | bytes 544 | tf_op jit(solution)/shard_map/ppermute | solution.py:245
  192.3 4.0 %collective-permute-done.49.refs_2_ = f32[128,1024]{1,0:T(8,128)S(1)} collective-permute-done((f32[128,1024]{1,0:T(8,128)S(1)}, f32[128,1024]{1,0:T(8,128)S(1)}, u32[]{:S(2)}, u32[]{:S(2)}) %collective-permute-start.49) | collective-permute-done | bytes 524320 | tf_op jit(solution)/shard_map/ppermute | solution.py:245
  199.2 2.5 %collective-permute-start.52 = (f32[1,128]{1,0:T(1,128)S(1)}, f32[1,128]{1,0:T(1,128)S(1)}, u32[]{:S(2)}, u32[]{:S(2)}) collective-permute-start(f32[1,128]{1,0:T(1,128)S(1)} %shard_map.119.refs_7_.refs_10_), channel_id=1, source_target_pairs={{0,16},{8,24},{16,0},{24,8},{1,17},{9,25},{17,1},{25,9},{2,18},{10... | collective-permute-start | bytes 1544 | tf_op jit(solution)/shard_map/ppermute | solution.py:245
  203.3 8.6 %collective-permute-done.52.refs_8_.refs_11_ = f32[1,128]{1,0:T(1,128)S(1)} collective-permute-done((f32[1,128]{1,0:T(1,128)S(1)}, f32[1,128]{1,0:T(1,128)S(1)}, u32[]{:S(2)}, u32[]{:S(2)}) %collective-permute-start.52) | collective-permute-done | bytes 544 | tf_op jit(solution)/shard_map/ppermute | solution.py:245
  (151 shorter events, 89.4 us)
Async XLA Ops:
  7.4 13.7 %collective-permute-start.5 = (f32[264,512]{1,0:T(8,128)S(1)}, f32[264,512]{1,0:T(8,128)S(1)}, u32[]{:S(2)}, u32[]{:S(2)}) collective-permute-start(f32[264,512]{1,0:T(8,128)S(1)} %get-tuple-element.174), channel_id=1, source_target_pairs={{0,4},{4,12},{8,0},{12,20},{16,8},{20,28},{24,16},{28,24},{1,5},{5... | collective-permute-start | bytes 1622024 | tf_op jit(solution)/shard_map/ppermute | solution.py:266
  9.8 13.1 %collective-permute-start.4 = (f32[264,512]{1,0:T(8,128)S(1)}, f32[264,512]{1,0:T(8,128)S(1)}, u32[]{:S(2)}, u32[]{:S(2)}) collective-permute-start(f32[264,512]{1,0:T(8,128)S(1)} %get-tuple-element.173.refs_9_), channel_id=1, source_target_pairs={{0,8},{4,0},{8,16},{12,4},{16,24},{20,12},{24,28},{28,20},{1,9},{5... | collective-permute-start | bytes 1622024 | tf_op jit(solution)/shard_map/ppermute | solution.py:266
  24.6 13.4 %collective-permute-start.7 = (f32[264,512]{1,0:T(8,128)}, f32[264,512]{1,0:T(8,128)}, u32[]{:S(2)}, u32[]{:S(2)}) collective-permute-start(f32[264,512]{1,0:T(8,128)} %get-tuple-element.178), channel_id=1, source_target_pairs={{0,4},{4,12},{8,0},{12,20},{16,8},{20,28},{24,16},{28,24},{1,5},{5... | collective-permute-start | bytes 1622024 | tf_op jit(solution)/shard_map/ppermute | solution.py:266
  26.4 13.4 %collective-permute-start.6 = (f32[264,512]{1,0:T(8,128)}, f32[264,512]{1,0:T(8,128)}, u32[]{:S(2)}, u32[]{:S(2)}) collective-permute-start(f32[264,512]{1,0:T(8,128)} %get-tuple-element.177.refs_10_.refs_7_), channel_id=1, source_target_pairs={{0,8},{4,0},{8,16},{12,4},{16,24},{20,12},{24,28},{28,20},{1,9},{5... | collective-permute-start | bytes 1622024 | tf_op jit(solution)/shard_map/ppermute | solution.py:266
  26.4 13.4 %collective-permute-start.2 = (f32[256,512]{1,0:T(8,128)}, f32[256,512]{1,0:T(8,128)S(1)}, u32[]{:S(2)}, u32[]{:S(2)}) collective-permute-start(f32[256,512]{1,0:T(8,128)} %get-tuple-element.171), channel_id=1, source_target_pairs={{0,4},{4,0},{1,5},{5,1},{2,6},{6,2},{3,7},{7,3},{8,12},{12,8},{9,1... | collective-permute-start | bytes 1572872 | tf_op jit(solution)/shard_map/ppermute | solution.py:245
  41.3 13.2 %collective-permute-start.10 = (f32[264,512]{1,0:T(8,128)S(1)}, f32[264,512]{1,0:T(8,128)S(1)}, u32[]{:S(2)}, u32[]{:S(2)}) collective-permute-start(f32[264,512]{1,0:T(8,128)S(1)} %get-tuple-element.188), channel_id=1, source_target_pairs={{0,4},{4,12},{8,0},{12,20},{16,8},{20,28},{24,16},{28,24},{1,5},{5... | collective-permute-start | bytes 1622024 | tf_op jit(solution)/shard_map/ppermute | solution.py:266
  43.1 13.0 %collective-permute-start.9 = (f32[264,512]{1,0:T(8,128)S(1)}, f32[264,512]{1,0:T(8,128)S(1)}, u32[]{:S(2)}, u32[]{:S(2)}) collective-permute-start(f32[264,512]{1,0:T(8,128)S(1)} %get-tuple-element.187.refs_12_.refs_8_.refs_6_.refs_1_), channel_id=1, source_target_pairs={{0,8},{4,0},{8,16},{12,4},{16,24},{20,12},{24,28},{28,20},{1,9},{5... | collective-permute-start | bytes 1622024 | tf_op jit(solution)/shard_map/ppermute | solution.py:266
  43.1 13.0 %collective-permute-start.1 = (f32[256,512]{1,0:T(8,128)S(1)}, f32[256,512]{1,0:T(8,128)S(1)}, u32[]{:S(2)}, u32[]{:S(2)}) collective-permute-start(f32[256,512]{1,0:T(8,128)S(1)} %copy-done.12), channel_id=1, source_target_pairs={{0,4},{4,0},{1,5},{5,1},{2,6},{6,2},{3,7},{7,3},{8,12},{12,8},{9,1... | collective-permute-start | bytes 1572872 | tf_op jit(solution)/shard_map/ppermute | solution.py:245
  57.8 12.9 %collective-permute-start.13 = (f32[264,512]{1,0:T(8,128)S(1)}, f32[264,512]{1,0:T(8,128)S(1)}, u32[]{:S(2)}, u32[]{:S(2)}) collective-permute-start(f32[264,512]{1,0:T(8,128)S(1)} %get-tuple-element.194), channel_id=1, source_target_pairs={{0,4},{4,12},{8,0},{12,20},{16,8},{20,28},{24,16},{28,24},{1,5},{5... | collective-permute-start | bytes 1622024 | tf_op jit(solution)/shard_map/ppermute | solution.py:266
  58.6 13.9 %collective-permute-start.12 = (f32[264,512]{1,0:T(8,128)S(1)}, f32[264,512]{1,0:T(8,128)S(1)}, u32[]{:S(2)}, u32[]{:S(2)}) collective-permute-start(f32[264,512]{1,0:T(8,128)S(1)} %get-tuple-element.193.refs_10_.refs_7_.refs_3_), channel_id=1, source_target_pairs={{0,8},{4,0},{8,16},{12,4},{16,24},{20,12},{24,28},{28,20},{1,9},{5... | collective-permute-start | bytes 1622024 | tf_op jit(solution)/shard_map/ppermute | solution.py:266
  74.2 13.1 %collective-permute-start.17 = (f32[264,512]{1,0:T(8,128)S(1)}, f32[264,512]{1,0:T(8,128)S(1)}, u32[]{:S(2)}, u32[]{:S(2)}) collective-permute-start(f32[264,512]{1,0:T(8,128)S(1)} %get-tuple-element.200), channel_id=1, source_target_pairs={{0,4},{4,12},{8,0},{12,20},{16,8},{20,28},{24,16},{28,24},{1,5},{5... | collective-permute-start | bytes 1622024 | tf_op jit(solution)/shard_map/ppermute | solution.py:266
  74.2 13.5 %collective-permute-start.16 = (f32[264,512]{1,0:T(8,128)S(1)}, f32[264,512]{1,0:T(8,128)S(1)}, u32[]{:S(2)}, u32[]{:S(2)}) collective-permute-start(f32[264,512]{1,0:T(8,128)S(1)} %get-tuple-element.199.refs_9_.refs_5_), channel_id=1, source_target_pairs={{0,8},{4,0},{8,16},{12,4},{16,24},{20,12},{24,28},{28,20},{1,9},{5... | collective-permute-start | bytes 1622024 | tf_op jit(solution)/shard_map/ppermute | solution.py:266
  88.8 14.5 %collective-permute-start.22 = (f32[272,512]{1,0:T(8,128)S(1)}, f32[272,512]{1,0:T(8,128)S(1)}, u32[]{:S(2)}, u32[]{:S(2)}) collective-permute-start(f32[272,512]{1,0:T(8,128)S(1)} %get-tuple-element.212), channel_id=1, source_target_pairs={{0,4},{4,12},{8,0},{12,20},{16,8},{20,28},{24,16},{28,24},{1,5},{5... | collective-permute-start | bytes 1671176 | tf_op jit(solution)/shard_map/ppermute | solution.py:266
  89.0 14.3 %collective-permute-start.21 = (f32[272,512]{1,0:T(8,128)S(1)}, f32[272,512]{1,0:T(8,128)S(1)}, u32[]{:S(2)}, u32[]{:S(2)}) collective-permute-start(f32[272,512]{1,0:T(8,128)S(1)} %get-tuple-element.211.refs_7_), channel_id=1, source_target_pairs={{0,8},{4,0},{8,16},{12,4},{16,24},{20,12},{24,28},{28,20},{1,9},{5... | collective-permute-start | bytes 1671176 | tf_op jit(solution)/shard_map/ppermute | solution.py:266
  107.5 16.9 %collective-permute-start.28 = (f32[776,512]{1,0:T(8,128)S(1)}, f32[776,512]{1,0:T(8,128)S(1)}, u32[]{:S(2)}, u32[]{:S(2)}) collective-permute-start(f32[776,512]{1,0:T(8,128)S(1)} %get-tuple-element.229), channel_id=1, source_target_pairs={{0,4},{4,0},{1,5},{5,1},{2,6},{6,2},{3,7},{7,3},{8,12},{12,8},{9,1... | collective-permute-start | bytes 4767752 | tf_op jit(solution)/shard_map/ppermute | solution.py:245
  110.5 13.5 %collective-permute-start.27 = (f32[264,512]{1,0:T(8,128)S(1)}, f32[264,512]{1,0:T(8,128)S(1)}, u32[]{:S(2)}, u32[]{:S(2)}) collective-permute-start(f32[264,512]{1,0:T(8,128)S(1)} %get-tuple-element.223), channel_id=1, source_target_pairs={{0,4},{4,12},{8,0},{12,20},{16,8},{20,28},{24,16},{28,24},{1,5},{5... | collective-permute-start | bytes 1622024 | tf_op jit(solution)/shard_map/ppermute | solution.py:266
  110.5 13.9 %collective-permute-start.26 = (f32[264,512]{1,0:T(8,128)S(1)}, f32[264,512]{1,0:T(8,128)S(1)}, u32[]{:S(2)}, u32[]{:S(2)}) collective-permute-start(f32[264,512]{1,0:T(8,128)S(1)} %get-tuple-element.222.refs_11_), channel_id=1, source_target_pairs={{0,8},{4,0},{8,16},{12,4},{16,24},{20,12},{24,28},{28,20},{1,9},{5... | collective-permute-start | bytes 1622024 | tf_op jit(solution)/shard_map/ppermute | solution.py:266
  125.1 18.8 %collective-permute-start.32 = (f32[280,512]{1,0:T(8,128)S(1)}, f32[280,512]{1,0:T(8,128)S(1)}, u32[]{:S(2)}, u32[]{:S(2)}) collective-permute-start(f32[280,512]{1,0:T(8,128)S(1)} %get-tuple-element.240), channel_id=1, source_target_pairs={{0,4},{4,12},{8,0},{12,20},{16,8},{20,28},{24,16},{28,24},{1,5},{5... | collective-permute-start | bytes 1720328 | tf_op jit(solution)/shard_map/ppermute | solution.py:266
  127.1 16.9 %collective-permute-start.34 = (f32[280,512]{1,0:T(8,128)S(1)}, f32[280,512]{1,0:T(8,128)S(1)}, u32[]{:S(2)}, u32[]{:S(2)}) collective-permute-start(f32[280,512]{1,0:T(8,128)S(1)} %get-tuple-element.255.refs_1_), channel_id=1, source_target_pairs={{0,2},{2,0},{1,3},{3,1},{4,6},{6,4},{5,7},{7,5},{8,10},{10,8},{9,1... | collective-permute-start | bytes 1720328 | tf_op jit(solution)/shard_map/ppermute | solution.py:492
  127.4 16.6 %collective-permute-start.31 = (f32[280,512]{1,0:T(8,128)S(1)}, f32[280,512]{1,0:T(8,128)S(1)}, u32[]{:S(2)}, u32[]{:S(2)}) collective-permute-start(f32[280,512]{1,0:T(8,128)S(1)} %get-tuple-element.239.refs_12_.refs_9_), channel_id=1, source_target_pairs={{0,8},{4,0},{8,16},{12,4},{16,24},{20,12},{24,28},{28,20},{1,9},{5... | collective-permute-start | bytes 1720328 | tf_op jit(solution)/shard_map/ppermute | solution.py:266
  131.7 12.2 %collective-permute-start.35 = (f32[136,1024]{1,0:T(8,128)S(1)}, f32[136,1024]{1,0:T(8,128)S(1)}, u32[]{:S(2)}, u32[]{:S(2)}) collective-permute-start(f32[136,1024]{1,0:T(8,128)S(1)} %get-tuple-element.260.refs_1_), channel_id=1, source_target_pairs={{0,1},{1,0},{2,3},{3,2},{4,5},{5,4},{6,7},{7,6},{8,9},{9,8},{10,11... | collective-permute-start | bytes 1671176 | tf_op jit(solution)/shard_map/ppermute | solution.py:245
  144.7 15.7 %collective-permute-start.37 = (f32[280,512]{1,0:T(8,128)S(1)}, f32[280,512]{1,0:T(8,128)S(1)}, u32[]{:S(2)}, u32[]{:S(2)}) collective-permute-start(f32[280,512]{1,0:T(8,128)S(1)} %get-tuple-element.254), channel_id=1, source_target_pairs={{0,4},{4,12},{8,0},{12,20},{16,8},{20,28},{24,16},{28,24},{1,5},{5... | collective-permute-start | bytes 1720328 | tf_op jit(solution)/shard_map/ppermute | solution.py:266
  145.6 14.8 %collective-permute-start.36 = (f32[280,512]{1,0:T(8,128)S(1)}, f32[280,512]{1,0:T(8,128)S(1)}, u32[]{:S(2)}, u32[]{:S(2)}) collective-permute-start(f32[280,512]{1,0:T(8,128)S(1)} %get-tuple-element.253.refs_14_.refs_10_.refs_7_), channel_id=1, source_target_pairs={{0,8},{4,0},{8,16},{12,4},{16,24},{20,12},{24,28},{28,20},{1,9},{5... | collective-permute-start | bytes 1720328 | tf_op jit(solution)/shard_map/ppermute | solution.py:266
  161.5 15.3 %collective-permute-start.41 = (f32[264,512]{1,0:T(8,128)S(1)}, f32[264,512]{1,0:T(8,128)S(1)}, u32[]{:S(2)}, u32[]{:S(2)}) collective-permute-start(f32[264,512]{1,0:T(8,128)S(1)} %get-tuple-element.275), channel_id=1, source_target_pairs={{0,4},{4,12},{8,0},{12,20},{16,8},{20,28},{24,16},{28,24},{1,5},{5... | collective-permute-start | bytes 1622024 | tf_op jit(solution)/shard_map/ppermute | solution.py:266
  161.5 15.3 %collective-permute-start.40 = (f32[264,512]{1,0:T(8,128)S(1)}, f32[264,512]{1,0:T(8,128)S(1)}, u32[]{:S(2)}, u32[]{:S(2)}) collective-permute-start(f32[264,512]{1,0:T(8,128)S(1)} %get-tuple-element.274.refs_12_.refs_8_.refs_1_), channel_id=1, source_target_pairs={{0,8},{4,0},{8,16},{12,4},{16,24},{20,12},{24,28},{28,20},{1,9},{5... | collective-permute-start | bytes 1622024 | tf_op jit(solution)/shard_map/ppermute | solution.py:266
  177.6 18.7 %collective-permute-start.45 = (f32[264,512]{1,0:T(8,128)S(1)}, f32[264,512]{1,0:T(8,128)S(1)}, u32[]{:S(2)}, u32[]{:S(2)}) collective-permute-start(f32[264,512]{1,0:T(8,128)S(1)} %get-tuple-element.286), channel_id=1, source_target_pairs={{0,4},{4,12},{8,0},{12,20},{16,8},{20,28},{24,16},{28,24},{1,5},{5... | collective-permute-start | bytes 1622024 | tf_op jit(solution)/shard_map/ppermute | solution.py:266
  179.3 17.0 %collective-permute-start.44 = (f32[264,512]{1,0:T(8,128)S(1)}, f32[264,512]{1,0:T(8,128)S(1)}, u32[]{:S(2)}, u32[]{:S(2)}) collective-permute-start(f32[264,512]{1,0:T(8,128)S(1)} %get-tuple-element.285.refs_10_.refs_3_), channel_id=1, source_target_pairs={{0,8},{4,0},{8,16},{12,4},{16,24},{20,12},{24,28},{28,20},{1,9},{5... | collective-permute-start | bytes 1622024 | tf_op jit(solution)/shard_map/ppermute | solution.py:266
  182.8 13.6 %collective-permute-start.49 = (f32[128,1024]{1,0:T(8,128)S(1)}, f32[128,1024]{1,0:T(8,128)S(1)}, u32[]{:S(2)}, u32[]{:S(2)}) collective-permute-start(f32[128,1024]{1,0:T(8,128)S(1)} %get-tuple-element.307.refs_1_), channel_id=1, source_target_pairs={{0,1},{1,0},{2,3},{3,2},{4,5},{5,4},{6,7},{7,6},{8,9},{9,8},{10,11... | collective-permute-start | bytes 1572872 | tf_op jit(solution)/shard_map/ppermute | solution.py:245
  197.2 14.7 %collective-permute-start.51 = (f32[264,512]{1,0:T(8,128)S(1)}, f32[264,512]{1,0:T(8,128)S(1)}, u32[]{:S(2)}, u32[]{:S(2)}) collective-permute-start(f32[264,512]{1,0:T(8,128)S(1)} %get-tuple-element.296), channel_id=1, source_target_pairs={{0,4},{4,12},{8,0},{12,20},{16,8},{20,28},{24,16},{28,24},{1,5},{5... | collective-permute-start | bytes 1622024 | tf_op jit(solution)/shard_map/ppermute | solution.py:266
  197.2 14.7 %collective-permute-start.50 = (f32[264,512]{1,0:T(8,128)S(1)}, f32[264,512]{1,0:T(8,128)S(1)}, u32[]{:S(2)}, u32[]{:S(2)}) collective-permute-start(f32[264,512]{1,0:T(8,128)S(1)} %get-tuple-element.295.refs_5_), channel_id=1, source_target_pairs={{0,8},{4,0},{8,16},{12,4},{16,24},{20,12},{24,28},{28,20},{1,9},{5... | collective-permute-start | bytes 1622024 | tf_op jit(solution)/shard_map/ppermute | solution.py:266
  198.6 13.3 %collective-permute-start.53 = (f32[128,1024]{1,0:T(8,128)S(1)}, f32[128,1024]{1,0:T(8,128)S(1)}, u32[]{:S(2)}, u32[]{:S(2)}) collective-permute-start(f32[128,1024]{1,0:T(8,128)S(1)} %shard_map.121.refs_1_), channel_id=1, source_target_pairs={{0,2},{2,0},{1,3},{3,1},{4,6},{6,4},{5,7},{7,5},{8,10},{10,8},{9,1... | collective-permute-start | bytes 1572872 | tf_op jit(solution)/shard_map/ppermute | solution.py:245
  199.2 12.6 %collective-permute-start.52 = (f32[1,128]{1,0:T(1,128)S(1)}, f32[1,128]{1,0:T(1,128)S(1)}, u32[]{:S(2)}, u32[]{:S(2)}) collective-permute-start(f32[1,128]{1,0:T(1,128)S(1)} %shard_map.119.refs_7_.refs_10_), channel_id=1, source_target_pairs={{0,16},{8,24},{16,0},{24,8},{1,17},{9,25},{17,1},{25,9},{2,18},{10... | collective-permute-start | bytes 1544 | tf_op jit(solution)/shard_map/ppermute | solution.py:245
  (37 other events, 296.4 us)
